TPU v7x, 256 devices: a whole 4x4x8 slice. The times are simulated.
256 devices in a mesh: sensor: 8 (over y, core), space: 32 (over z, x).
Axes of the slice: x: 4, y: 4, z: 8, core: 2. Of those that a mesh axis runs over, the one named last changes fastest.
Arguments:
- jacobian: float32 [512, 131072], P('space', 'sensor'), as said below
- residual: float32 [131072], P('sensor'), may hold values from -6 to 6
- damping: float32 [1], replicated, may hold values from 0.3 to 3
Outputs:
- update: float32 [512], replicated
Inputs may be any that keep to these rules, and one draw needn't show every extreme that they name: `jacobian`: every column block of the Jacobian has full rank over any 512 observations, which number at least the parameters; the entries are real-valued with row and column scales that vary.
All inputs are finite; a program needn't handle non-finite values.
Results may differ from a plain program's by a relative error of at most 0.00011.
Values sent between devices are 32-bit elements; how exact they have to be, the bound alone decides.
A program may use at most 64 MiB of HBM per device.

v0:
```python
import jax
import jax.numpy as jnp
from jax import lax
from jax.sharding import PartitionSpec as P


def per_device(jacobian, residual, damping):
    high = lax.Precision.HIGHEST
    columns = jacobian.shape[0]
    groups = lax.axis_size("space")
    params_all = columns * groups
    part_grad = jnp.dot(jacobian, residual, precision=high)
    grad_local = lax.dynamic_update_slice(
        jnp.zeros((params_all,), jnp.float32), part_grad, (lax.axis_index("space") * columns,)
    )
    panel_t = lax.all_to_all(jacobian, "space", split_axis=1, concat_axis=0, tiled=True)
    gram_local = lax.dot_general(panel_t, panel_t, (((1,), (1,)), ((), ())), precision=high)
    gram_all, grad_all = lax.psum((gram_local, grad_local), ("sensor", "space"))
    damped = gram_all + damping[0] * jnp.diag(jnp.diag(gram_all))
    factor = jnp.linalg.cholesky(damped)
    return -jax.scipy.linalg.cho_solve((factor, True), grad_all)


def solution(mesh):
    placed = (P("space", "sensor"), P("sensor"), P())
    return jax.shard_map(per_device, mesh=mesh, in_specs=placed, out_specs=P(), check_vma=False)
```

profile of v0, /device:TPU:1, one launch (start us, length us, event | category | flops | bytes accessed | tf_op | source)
XLA Modules:
  0.0 455.3 jit_solution(10162979541836182805)
XLA Ops:
  6.5 1.3 copy.52
  7.9 37.9 %all_to_all.19 = f32[16,32,512]{2,0,1:T(8,128)S(1)} all-to-all(f32[16,32,512]{2,0,1:T(8,128)S(1)} %bitcast.158), channel_id=1, replica_groups=mesh['sensor'=8,'space'=32] {'space'}, dimensions={1} | all-to-all | bytes 2097152 | tf_op jit(solution)/shard_map/all_to_all | solution.py:16
  45.8 2.9 fusion.57
  49.4 0.5 copy-done.2
  49.9 1.3 convolution_bitcast_fusion
  51.2 0.2 dynamic_update_slice.3
  51.4 77.4 %psum.15 = f32[512]{0:T(512)S(1)} all-reduce(f32[512]{0:T(512)S(1)} %dynamic_update_slice.3), channel_id=1, replica_groups=mesh['sensor'=8,'space'=32] {'sensor','space'}, use_global_device_ids=true, to_apply=%region_9.10 | all-reduce | flops 512 | bytes 4096 | tf_op jit(solution)/shard_map/psum | solution.py:18
  128.9 174.0 %all-reduce.3.cloned.1.call-done = f32[512,512]{0,1:T(8,128)} async-done(((f32[512,512]{0,1:T(8,128)}), f32[512,512]{0,1:T(8,128)}) %all-reduce.3.cloned.1.call-update) | async-done | bytes 1048592 | tf_op jit(solution)/shard_map/psum | solution.py:18
  302.9 8.6 %gather_fusion = f32[512]{0:T(512)S(1)} fusion(f32[512,512]{0,1:T(8,128)} %all-reduce.3.cloned.1.call-done, s32[512]{0:T(512)S(1)} %bitcast.155), kind=kCustom, calls=%fused_computation | custom fusion | bytes 8192 | tf_op jit(solution)/shard_map/jit(_diag)/jit(diagonal)/cond/branch_0_fun/gather | solution.py:19
  311.5 0.1 multiply_add_fusion
  311.6 0.3 copy.37
  312.0 0.2 fusion.12
  312.2 11.7 %cholesky.103 = f32[128,128]{1,0:T(8,128)S(1)} custom-call(f32[128,128]{1,0:T(8,128)S(1)} %cholesky.263), custom_call_target="Cholesky" | custom-call | tf_op jit(solution)/shard_map/jit(cholesky)/cholesky | solution.py:20
  323.9 0.1 copy.38
  324.1 9.8 %custom-call.34 = f32[1,128,128]{1,2,0:T(8,128)S(1)} custom-call(f32[1,128,128]{2,1,0:T(8,128)S(1)} %get-tuple-element.44), custom_call_target="InvertDiagBlocksLowerTriangular" | custom-call | tf_op jit(solution)/shard_map/jit(cholesky)/cholesky | solution.py:20
  333.9 0.3 fusion.17
  334.2 0.1 copy.39
  334.3 0.3 convolution_subtract_fusion
  334.7 11.7 %cholesky.215 = f32[128,128]{1,0:T(8,128)S(1)} custom-call(f32[128,128]{1,0:T(8,128)S(1)} %cholesky.267), custom_call_target="Cholesky" | custom-call | tf_op jit(solution)/shard_map/jit(cholesky)/cholesky | solution.py:20
  346.4 0.1 copy.40
  346.5 0.1 cholesky.222
  346.7 10.0 %custom-call.35 = f32[1,128,128]{1,2,0:T(8,128)S(1)} custom-call(f32[1,128,128]{2,1,0:T(8,128)S(1)} %get-tuple-element.42), custom_call_target="InvertDiagBlocksLowerTriangular" | custom-call | tf_op jit(solution)/shard_map/jit(cholesky)/cholesky | solution.py:20
  356.7 0.3 convolution_dynamic-update-slice_fusion
  357.0 0.6 convolution_subtract_fusion.1
  357.6 11.7 %cholesky.236 = f32[128,128]{1,0:T(8,128)S(1)} custom-call(f32[128,128]{1,0:T(8,128)S(1)} %cholesky.272), custom_call_target="Cholesky" | custom-call | tf_op jit(solution)/shard_map/jit(cholesky)/cholesky | solution.py:20
  369.4 0.1 copy.42
  369.5 9.8 %custom-call.36 = f32[1,128,128]{1,2,0:T(8,128)S(1)} custom-call(f32[1,128,128]{2,1,0:T(8,128)S(1)} %get-tuple-element.40), custom_call_target="InvertDiagBlocksLowerTriangular" | custom-call | tf_op jit(solution)/shard_map/jit(cholesky)/cholesky | solution.py:20
  379.3 0.3 convolution_dynamic-update-slice_fusion.1
  379.6 0.5 convolution_subtract_fusion.2
  380.1 11.9 %cholesky.253 = f32[128,128]{1,0:T(8,128)S(1)} custom-call(f32[128,128]{1,0:T(8,128)S(1)} %convolution_subtract_fusion.2), custom_call_target="Cholesky" | custom-call | tf_op jit(solution)/shard_map/jit(cholesky)/cholesky | solution.py:20
  392.1 0.1 copy.44
  392.2 0.7 compare_reduce_fusion.1
  392.9 0.6 compare_reduce_fusion
  393.6 0.7 compare_reduce_fusion.2
  396.8 0.1 select_select_fusion
  396.9 8.6 %while.1 = (s32[]{:T(128)}, f32[512,512]{0,1:T(8,128)S(1)}, s32[4,2]{0,1:T(2,128)S(1)}, f32[4,128,128]{2,1,0:T(8,128)S(1)}, s32[]{:T(128)}) while((s32[]{:T(128)}, f32[512,512]{0,1:T(8,128)S(1)}, s32[4,2]{0,1:T(2,128)S(1)}, f32[4,128,128]{2,1,0:T(8,128)S(1)}, s32[]{:T(128)}) %tuple.27), condition=%wide.while_cond, body=%wide.while_body.sunk | while | flops 2 | bytes 393329 | solution.py:21
  397.0 0.6 fusion.72
  397.6 1.3 dynamic-slice.7
  399.0 0.1 copy.54
  399.2 0.6 fusion.72
  399.8 1.3 dynamic-slice.7
  401.1 0.1 copy.54
  401.3 0.6 fusion.72
  401.9 1.3 dynamic-slice.7
  403.3 0.1 copy.54
  403.5 0.6 fusion.72
  404.1 1.3 dynamic-slice.7
  405.4 0.1 copy.54
  405.5 39.3 %custom-call.37 = f32[4,128,128]{1,2,0:T(8,128)S(1)} custom-call(f32[4,128,128]{2,1,0:T(8,128)S(1)} %get-tuple-element.12), custom_call_target="InvertDiagBlocksLowerTriangular" | custom-call | tf_op jit(solution)/shard_map/jit(_cho_solve)/triangular_solve | solution.py:21
  444.9 0.2 fusion.30
  445.0 0.2 fusion.5
  445.2 0.2 fusion.31
  445.4 0.2 fusion.6
  445.5 0.2 fusion.32
  445.7 0.2 fusion.11
  446.0 0.2 convolution_bitcast_fusion.7
  446.1 0.2 convolution_bitcast_fusion.6
  446.3 0.2 fusion.2
  446.6 0.2 convolution_bitcast_fusion.4
  446.8 0.2 fusion.7
  447.0 0.2 convolution_bitcast_fusion.2
  447.2 0.3 fusion.9
  447.5 0.2 convolution_bitcast_fusion.1
  447.8 0.6 maximum_negate_fusion
  (31 shorter events, 0.6 us)
Async XLA Ops:
  6.5 42.9 %copy-start = (f32[16384]{0:T(1024)S(1)}, f32[16384]{0:T(1024)}, u32[]{:S(2)}) copy-start(f32[16384]{0:T(1024)} %param.4) | copy-start | bytes 196612
  6.5 296.3 %all-reduce.3.cloned.1.call-start = ((), (), s32[]{:S(2)}) async-start(), calls=%async_computation.1 | async-start | bytes 2097152 | tf_op jit(solution)/shard_map/psum | solution.py:18
  48.7 1.2 copy-start.2
  302.8 8.6 %copy-start.1 = (f32[512,512]{0,1:T(8,128)S(1)}, f32[512,512]{0,1:T(8,128)}, u32[]{:S(2)}) copy-start(f32[512,512]{0,1:T(8,128)} %all-reduce.3.cloned.1.call-done) | copy-start | bytes 3145732
Sparse Core Ops, SparseCore 0:
  48.8 253.9 all-reduce.2
where the time goes:
time: 456 us; the launch traced here: 455 us
  waiting for transfers between devices  174 us (38%)
  other arithmetic  119 us (26%)
  blocking collectives  115 us (25%)
  local copies, waits for them, and re-layouts  20.1 us (4%)
  between operations  16.9 us (4%)
  matrix products  9.47 us (2%)
    psum x1, waiting for transfers between devices, per_device(): gram_all, grad_all = lax.psum((gram_local, grad_local), ('sensor', 'space'))  174 us
    another operation x14, other arithmetic, per_device(): factor = jnp.linalg.cholesky(damped)  78.9 us
    psum x1, blocking collectives, per_device(): gram_all, grad_all = lax.psum((gram_local, grad_local), ('sensor', 'space'))  77.4 us
    another operation x3, other arithmetic, per_device(): return -jax.scipy.linalg.cho_solve((factor, True), grad_all)  39.4 us
    all_to_all x1, blocking collectives, per_device(): lax.all_to_all(jacobian, 'space', split_axis=1, concat_axis=0, tiled=True)  37.9 us
  transfers between devices with their start and end apart: 1, of which 1 were waited for; matrix products, arithmetic and copies ran while one was open for 0% of the time, Pallas kernels for 0%

commit v1 on v0

v1 whole, which is shorter than its diff:
```python
import functools
import jax
import jax.numpy as jnp
from jax import lax
from jax.experimental import pallas as pl
from jax.experimental.pallas import tpu as pltpu
from jax.sharding import PartitionSpec as P

LANES = 128
MESH = pl.DeviceIdType.MESH
YS, CORES, ZS, XS = 4, 2, 8, 4


def regroup_kernel(j_ref, r_ref, out_ref, panel, pack, core_rx, y_rx, y_sum, z_rx, x_all, own_sem,
                   a2a_send, a2a_recv, core_send, core_recv, y_send, y_recv, z_send, z_recv, x_send, x_recv,
                   zg_send, zg_recv, yg_send, yg_recv, cg_send, cg_recv):
    sensor, space = lax.axis_index("sensor"), lax.axis_index("space")
    y, core = sensor // CORES, sensor % CORES
    z, x = space // XS, space % XS
    spaces = ZS * XS
    rows = j_ref.shape[0]
    cols = j_ref.shape[1] // spaces
    params = rows * spaces
    blocks = params // LANES

    def on_space(dz, dx):
        return lax.rem(z + dz + ZS, ZS) * XS + lax.rem(x + dx + XS, XS)

    def on_y(d):
        return lax.rem(y + d + YS, YS) * CORES + core

    other_core = y * CORES + (1 - core)

    own = pltpu.make_async_copy(
        j_ref.at[:, pl.ds(pl.multiple_of(space * cols, cols), cols)],
        panel.at[pl.ds(pl.multiple_of(space * rows, rows), rows), :],
        own_sem,
    )
    own.start()

    barrier = pltpu.get_barrier_semaphore()

    def greet(d, carry):
        pl.semaphore_signal(barrier, inc=1, device_id={"space": lax.rem(space + d, spaces)}, device_id_type=MESH)
        return carry

    lax.fori_loop(1, spaces, greet, 0)
    pl.semaphore_signal(barrier, inc=1, device_id={"sensor": other_core}, device_id_type=MESH)
    for d in range(1, YS):
        pl.semaphore_signal(barrier, inc=1, device_id={"sensor": on_y(d)}, device_id_type=MESH)
    pl.semaphore_wait(barrier, spaces - 1 + 1 + YS - 1)

    def regroup(d, sign):
        to = on_space(sign * (d // XS), sign * lax.rem(d, XS))
        src_of = to if sign == 1 else space
        at = space if sign == 1 else to
        return pltpu.make_async_remote_copy(
            src_ref=j_ref.at[:, pl.ds(pl.multiple_of(src_of * cols, cols), cols)],
            dst_ref=panel.at[pl.ds(pl.multiple_of(at * rows, rows), rows), :],
            send_sem=a2a_send.at[d],
            recv_sem=a2a_recv.at[at],
            device_id={"space": to},
            device_id_type=MESH,
        )

    def start(d, carry):
        regroup(d, 1).start()
        return carry

    def arrive(d, carry):
        regroup(d, -1).wait_recv()
        return carry

    def sent(d, carry):
        regroup(d, 1).wait_send()
        return carry

    lax.fori_loop(1, spaces, start, 0)
    pack[...] = jnp.zeros_like(pack)
    own.wait()
    lax.fori_loop(1, spaces, arrive, 0)

    high = lax.Precision.HIGHEST
    across = (((1,), (1,)), ((), ()))
    at = 0
    for b in range(blocks):
        left = panel[b * LANES : (b + 1) * LANES, :]
        strip = lax.dot_general(left, panel[b * LANES :, :], across, precision=high, preferred_element_type=jnp.float32)
        for c in range(blocks - b):
            pack[at : at + LANES, :] = strip[:, c * LANES : (c + 1) * LANES]
            at += LANES
    pieces = cols // LANES
    r_row = jnp.concatenate([r_ref[pl.ds(space * pieces + i, 1), :] for i in range(pieces)], axis=1)
    g = lax.dot_general(jnp.broadcast_to(r_row, (8, cols)), panel[...], across, precision=high, preferred_element_type=jnp.float32)
    for b in range(blocks):
        pack[at + b : at + b + 1, :] = g[0:1, b * LANES : (b + 1) * LANES]

    half = pack.shape[0] // CORES
    quarter = half // YS
    piece = quarter // ZS

    def remote(src, dst, send, recv, target):
        return pltpu.make_async_remote_copy(src_ref=src, dst_ref=dst, send_sem=send, recv_sem=recv, device_id=target, device_id_type=MESH)

    def run(copies):
        for c in copies:
            c.start()
        for c in copies:
            c.wait()

    mine = pl.multiple_of(core * half, half)
    theirs = pl.multiple_of((1 - core) * half, half)
    run([remote(pack.at[pl.ds(theirs, half), :], core_rx, core_send, core_recv, {"sensor": other_core})])
    pack[pl.ds(mine, half), :] += core_rx[...]

    def y_part(yy):
        return pl.ds(pl.multiple_of(mine + yy * quarter, quarter), quarter)

    run([
        remote(pack.at[y_part(lax.rem(y + d, YS)), :], y_rx.at[d - 1], y_send.at[d - 1], y_recv.at[d - 1], {"sensor": on_y(d)})
        for d in range(1, YS)
    ])
    y_sum[...] = pack[y_part(y), :] + y_rx[0] + y_rx[1] + y_rx[2]

    def z_part(zz, base=0):
        return pl.ds(pl.multiple_of(base + zz * piece, piece), piece)

    run([
        remote(y_sum.at[z_part(lax.rem(z + d, ZS)), :], z_rx.at[d - 1], z_send.at[d - 1], z_recv.at[d - 1], {"space": on_space(d, 0)})
        for d in range(1, ZS)
    ])
    total = y_sum[z_part(z), :]
    for d in range(ZS - 1):
        total = total + z_rx[d]
    x_all[x] = total
    run([
        remote(x_all.at[x], x_all.at[x], x_send.at[d - 1], x_recv.at[d - 1], {"space": on_space(0, d)})
        for d in range(1, XS)
    ])
    total = x_all[0]
    for d in range(1, XS):
        total = total + x_all[d]
    base = mine + y * quarter
    out_ref[z_part(z, base), :] = total
    run([
        remote(out_ref.at[z_part(z, base), :], out_ref.at[z_part(z, base), :], zg_send.at[d - 1], zg_recv.at[d - 1], {"space": on_space(d, 0)})
        for d in range(1, ZS)
    ])
    run([
        remote(out_ref.at[y_part(y), :], out_ref.at[y_part(y), :], yg_send.at[d - 1], yg_recv.at[d - 1], {"sensor": on_y(d)})
        for d in range(1, YS)
    ])
    run([remote(out_ref.at[pl.ds(mine, half), :], out_ref.at[pl.ds(mine, half), :], cg_send, cg_recv, {"sensor": other_core})])
    lax.fori_loop(1, spaces, sent, 0)


def normal_matrix(jacobian, residual):
    rows, local = jacobian.shape
    spaces = ZS * XS
    params, cols = rows * spaces, local // spaces
    blocks = params // LANES
    packed = (blocks * (blocks + 1) // 2 + 1) * LANES
    unit = CORES * YS * ZS * 8
    packed = -(-packed // unit) * unit
    half = packed // CORES
    quarter = half // YS
    piece = quarter // ZS
    f32, dma = jnp.float32, pltpu.SemaphoreType.DMA
    return pl.pallas_call(
        regroup_kernel,
        out_shape=jax.ShapeDtypeStruct((packed, LANES), f32),
        in_specs=[pl.BlockSpec(memory_space=pl.ANY), pl.BlockSpec(memory_space=pltpu.VMEM)],
        out_specs=pl.BlockSpec(memory_space=pltpu.VMEM),
        scratch_shapes=[
            pltpu.VMEM((params, cols), f32),
            pltpu.VMEM((packed, LANES), f32),
            pltpu.VMEM((half, LANES), f32),
            pltpu.VMEM((YS - 1, quarter, LANES), f32),
            pltpu.VMEM((quarter, LANES), f32),
            pltpu.VMEM((ZS - 1, piece, LANES), f32),
            pltpu.VMEM((XS, piece, LANES), f32),
            dma,
            dma((spaces,)), dma((spaces,)),
            dma, dma,
            dma((YS - 1,)), dma((YS - 1,)),
            dma((ZS - 1,)), dma((ZS - 1,)),
            dma((XS - 1,)), dma((XS - 1,)),
            dma((ZS - 1,)), dma((ZS - 1,)),
            dma((YS - 1,)), dma((YS - 1,)),
            dma, dma,
        ],
        compiler_params=pltpu.CompilerParams(collective_id=0, has_side_effects=True, vmem_limit_bytes=32 << 20),
    )(jacobian, residual.reshape(-1, LANES))


SLAB = 32


def block_at(b, c, blocks):
    return b * blocks - b * (b - 1) // 2 + (c - b)


def split3(v):
    hi = v.astype(jnp.bfloat16)
    rest = v - hi.astype(jnp.float32)
    mid = rest.astype(jnp.bfloat16)
    low = (rest - mid.astype(jnp.float32)).astype(jnp.bfloat16)
    return hi, mid, low


def solve_kernel(blocks, packed, damping, x_ref, mat):
    tri = blocks * (blocks + 1) // 2
    wide = blocks + 1
    eye = lax.broadcasted_iota(jnp.int32, (LANES, LANES), 0) == lax.broadcasted_iota(jnp.int32, (LANES, LANES), 1)
    lam = damping[0]
    scale_rows, scale_cols = [], []
    for b in range(blocks):
        at = block_at(b, b, blocks) * LANES
        diag = jnp.where(eye, packed[at : at + LANES, :], 0.0)
        scale_rows.append(lax.rsqrt(jnp.sum(diag, axis=0, keepdims=True)))
        scale_cols.append(lax.rsqrt(jnp.sum(diag, axis=1, keepdims=True)))
    for b in range(blocks):
        for c in range(b, blocks):
            at = block_at(b, c, blocks) * LANES
            v = packed[at : at + LANES, :] * scale_cols[b] * scale_rows[c]
            if b == c:
                v = jnp.where(eye, 1.0 + lam, v)
            mat[b * LANES : (b + 1) * LANES, c * LANES : (c + 1) * LANES] = v
        g_row = packed[tri * LANES + b : tri * LANES + b + 1, :] * scale_rows[b]
        g_col = jnp.sum(jnp.where(eye, g_row, 0.0), axis=1, keepdims=True)
        mat[b * LANES : (b + 1) * LANES, blocks * LANES :] = jnp.broadcast_to(g_col, (LANES, LANES))

    lane = lax.broadcasted_iota(jnp.int32, (8, LANES), 1)
    sub = lax.broadcasted_iota(jnp.int32, (8, LANES), 0)

    def row(v, i):
        return jnp.broadcast_to(v[i : i + 1, :], (8, LANES))

    def slab_step(b, inner):
        tiles = list(range(b, wide))
        top = b * LANES + inner * SLAB
        if not isinstance(top, int):
            top = pl.multiple_of(top, SLAB)
        groups = SLAB // 8
        s = [[mat[pl.ds(top + 8 * g, 8), t * LANES : (t + 1) * LANES] for t in tiles] for g in range(groups)]
        before = [[v for v in r] for r in s]
        for g in range(groups):
            shift = inner * SLAB + 8 * g
            rolled = [pltpu.roll(s[i][0], (LANES - shift) % LANES, 1) for i in range(groups)]
            cols = [[jnp.broadcast_to(rolled[i][:, q : q + 1], (8, LANES)) for q in range(8)] for i in range(groups)]
            for p in range(0, 8, 2):
                at, bt, ct = row(cols[g][p], p), row(cols[g][p + 1], p), row(cols[g][p + 1], p + 1)
                det = at * ct - bt * bt
                r = pl.reciprocal(det, approx=True)
                r = r * (2.0 - det * r)
                r = r * (2.0 - det * r)
                av, bv, cv = at * r, bt * r, ct * r

                def eliminate(z):
                    z0, z1 = row(z[g], p), row(z[g], p + 1)
                    u0 = cv * z0 - bv * z1
                    u1 = av * z1 - bv * z0
                    out = []
                    for i in range(groups):
                        v = z[i] - cols[i][p] * u0 - cols[i][p + 1] * u1
                        if i == g:
                            v = jnp.where(sub == p, u0, jnp.where(sub == p + 1, u1, v))
                        out.append(v)
                    return out

                for q in range(p + 2, 8):
                    new = eliminate([cols[i][q] for i in range(groups)])
                    for i in range(groups):
                        cols[i][q] = new[i]
                for t in range(len(tiles)):
                    new = eliminate([s[i][t] for i in range(groups)])
                    for i in range(groups):
                        s[i][t] = new[i]
        full = lambda a: jnp.concatenate([jnp.concatenate(r, axis=1) for r in a], axis=0)
        u = full(s)
        x = full(before)
        mat[pl.ds(top, SLAB), b * LANES :] = u
        keep = lax.broadcasted_iota(jnp.int32, x.shape, 1) >= (inner + 1) * SLAB
        x = jnp.where(keep, x, 0.0)
        xh, xm, xl = split3(x[:, : (blocks - b) * LANES])
        uh, um, ul = split3(u)
        left = jnp.concatenate([xh, xh, xm, xh, xl, xm], axis=0)
        right = jnp.concatenate([uh, um, uh, ul, uh, um], axis=0)
        for i in range(b, blocks):
            o = (i - b) * LANES
            prod = lax.dot_general(left[:, o : o + LANES], right[:, o:], (((0,), (0,)), ((), ())), preferred_element_type=jnp.float32)
            mat[i * LANES : (i + 1) * LANES, i * LANES :] -= prod

    for b in range(blocks):
        def body(inner, carry, b=b):
            slab_step(b, inner)
            return carry

        lax.fori_loop(0, LANES // SLAB, body, 0)

    per = LANES // SLAB
    xs = [jnp.zeros((1, LANES), jnp.float32) for _ in range(blocks)]
    for k in reversed(range(blocks * per)):
        b, inner = divmod(k, per)
        u = mat[k * SLAB : (k + 1) * SLAB, :]
        acc = None
        for t in range(b, blocks):
            if t == blocks - 1 and k == blocks * per - 1:
                continue
            term = u[:, t * LANES : (t + 1) * LANES] * xs[t]
            acc = term if acc is None else acc + term
        col = u[:, blocks * LANES :]
        if acc is not None:
            col = col - jnp.sum(acc, axis=1, keepdims=True)
        pick = lax.broadcasted_iota(jnp.int32, (SLAB, LANES), 1) == lax.broadcasted_iota(jnp.int32, (SLAB, LANES), 0) + inner * SLAB
        xs[b] = xs[b] + jnp.sum(jnp.where(pick, col, 0.0), axis=0, keepdims=True)
    for b in range(blocks):
        x_ref[b : b + 1, :] = -(xs[b] * scale_rows[b])


def solve(packed, damping, params):
    blocks = params // LANES
    out = pl.pallas_call(
        functools.partial(solve_kernel, blocks),
        out_shape=jax.ShapeDtypeStruct((blocks, LANES), jnp.float32),
        in_specs=[pl.BlockSpec(memory_space=pltpu.VMEM), pl.BlockSpec(memory_space=pltpu.SMEM)],
        out_specs=pl.BlockSpec(memory_space=pltpu.VMEM),
        scratch_shapes=[pltpu.VMEM((params, params + LANES), jnp.float32)],
        compiler_params=pltpu.CompilerParams(vmem_limit_bytes=32 << 20),
    )(packed, damping)
    return out.reshape(params)


def per_device(jacobian, residual, damping):
    params = jacobian.shape[0] * ZS * XS
    return solve(normal_matrix(jacobian, residual), damping, params)


def solution(mesh):
    placed = (P("space", "sensor"), P("sensor"), P())
    return jax.shard_map(per_device, mesh=mesh, in_specs=placed, out_specs=P(), check_vma=False)
```

time: 456 us -> 101 us (0.22)
  waiting for transfers between devices: 174 us -> 0 us
  other arithmetic: 119 us -> 0 us
  blocking collectives: 115 us -> 0 us
  Pallas kernels: 0 us -> 98.3 us
  local copies, waits for them, and re-layouts: 20.1 us -> 2.06 us
  between operations: 16.9 us -> 0.67 us
  matrix products: 9.47 us -> 0 us
    psum x1 -> x0, waiting for transfers between devices: 174 us -> none  [per_device(): gram_all, grad_all = lax.psum((gram_local, grad_local), ('sensor', 'space'))]
    another operation x17 -> x0, other arithmetic: 118 us -> none  [the longest x14 78.9 us: per_device(): factor = jnp.linalg.cholesky(damped)]
    pallas_call x0 -> x2, Pallas kernels: none -> 98.3 us  [the longest x1 71.2 us: normal_matrix(): pl.pallas_call(regroup_kernel, out_shape=jax.ShapeDtypeStruct((packed, LA...]
    psum x1 -> x0, blocking collectives: 77.4 us -> none  [per_device(): gram_all, grad_all = lax.psum((gram_local, grad_local), ('sensor', 'space'))]
    all_to_all x1 -> x0, blocking collectives: 37.9 us -> none  [per_device(): lax.all_to_all(jacobian, 'space', split_axis=1, concat_axis=0, tiled=True)]
    another operation x34 -> x0, local copies, waits for them, and re-layouts: 9.14 us -> none
    gather x1 -> x0, local copies, waits for them, and re-layouts: 8.6 us -> none  [per_device(): damped = gram_all + damping[0] * jnp.diag(jnp.diag(gram_all))]
    another operation x20 -> x0, matrix products: 5.24 us -> none  [the longest x14 2.91 us: per_device(): return -jax.scipy.linalg.cho_solve((factor, True), grad_all)]
  transfers between devices with their start and end apart: 1 -> 0, of which waited for: 1 -> 0; matrix products, arithmetic and copies ran while one was open for 0% -> 0% of each run, Pallas kernels for 0% -> 0%
where the time goes in v1:
time: 101 us
  Pallas kernels  98.3 us (97%)
  local copies, waits for them, and re-layouts  2.06 us (2%)
    pallas_call x1, Pallas kernels, normal_matrix(): pl.pallas_call(regroup_kernel, out_shape=jax.ShapeDtypeStruct((packed, LA...  71.2 us
    pallas_call x1, Pallas kernels, solve(): pl.pallas_call(functools.partial(solve_kernel, blocks), out_shape=jax.Sha...  27.1 us
    unnamed x4, local copies, waits for them, and re-layouts  2.06 us

profile of v1, /device:TPU:1, one launch (start us, length us, event | category | flops | bytes accessed | tf_op | source)
XLA Modules:
  0.0 101.1 jit_solution(3960415359946719424)
XLA Ops:
  0.7 0.0 copy-start
  0.7 1.2 %copy-done = f32[16,16384]{1,0:T(8,128)S(1)} copy-done((f32[16,16384]{1,0:T(8,128)S(1)}, f32[16,16384]{1,0:T(8,128)}, u32[]{:S(2)}) %copy-start) | copy-done | bytes 1048600
  1.9 0.0 copy-start.1
  1.9 0.8 copy-done.1
  2.7 71.2 %shard_map.37.packed = f32[1536,128]{1,0:T(8,128)S(1)} custom-call(f32[16,16384]{1,0:T(8,128)S(1)} %copy-done, f32[128,128]{1,0:T(8,128)S(1)} %bitcast.2), custom_call_target="tpu_custom_call" | custom-call | tf_op jit(solution)/shard_map/pallas_call | solution.py:169
  73.9 27.1 %shard_map.38 = f32[4,128]{1,0:T(4,128)} custom-call(f32[1536,128]{1,0:T(8,128)S(1)} %shard_map.37.packed, f32[1]{0:T(128)S(6)} %copy.4.damping), custom_call_target="tpu_custom_call" | custom-call | tf_op jit(solution)/shard_map/pallas_call | solution.py:323
Async XLA Ops:
  0.7 1.2 %copy-start = (f32[16,16384]{1,0:T(8,128)S(1)}, f32[16,16384]{1,0:T(8,128)}, u32[]{:S(2)}) copy-start(f32[16,16384]{1,0:T(8,128)} %j_ref.1) | copy-start | bytes 3145732
  1.9 0.8 copy-start.1

commit v2 on v1

v2 whole, which is shorter than its diff:
```python
import functools
import jax
import jax.numpy as jnp
from jax import lax
from jax.experimental import pallas as pl
from jax.experimental.pallas import tpu as pltpu
from jax.sharding import PartitionSpec as P

LANES = 128
MESH = pl.DeviceIdType.MESH
YS, CORES, ZS, XS = 4, 2, 8, 4
CHUNKS = 4
SLAB = 64
PANEL = 16


def split3(v):
    hi = v.astype(jnp.bfloat16)
    rest = v - hi.astype(jnp.float32)
    mid = rest.astype(jnp.bfloat16)
    low = (rest - mid.astype(jnp.float32)).astype(jnp.bfloat16)
    return hi, mid, low


def regroup_kernel(j_ref, r_ref, out_ref, panel, r_own, pack, core_rx, y_rx, y_sum, z_rx, x_all, own_sem, r_sem,
                   a2a_send, a2a_recv, core_send, core_recv, y_send, y_recv, z_send, z_recv, x_send, x_recv,
                   zg_send, zg_recv, yg_send, yg_recv, cg_send, cg_recv):
    sensor, space = lax.axis_index("sensor"), lax.axis_index("space")
    y, core = sensor // CORES, sensor % CORES
    z, x = space // XS, space % XS
    spaces = ZS * XS
    rows = j_ref.shape[0]
    cols = j_ref.shape[1] // spaces
    params = rows * spaces
    blocks = params // LANES
    depth = cols // CHUNKS

    def on_space(dz, dx):
        return lax.rem(z + dz + ZS, ZS) * XS + lax.rem(x + dx + XS, XS)

    def on_y(d):
        return lax.rem(y + d + YS, YS) * CORES + core

    other_core = y * CORES + (1 - core)
    my_rows = pl.ds(pl.multiple_of(space * rows, rows), rows)

    def piece_of(device, chunk):
        return j_ref.at[:, pl.ds(pl.multiple_of(device * cols + chunk * depth, depth), depth)]

    own = [pltpu.make_async_copy(piece_of(space, c), panel.at[c, my_rows, :], own_sem.at[c]) for c in range(CHUNKS)]
    for copy in own:
        copy.start()
    r_copy = pltpu.make_async_copy(r_ref.at[space], r_own, r_sem)
    r_copy.start()

    barrier = pltpu.get_barrier_semaphore()

    def greet(d, carry):
        pl.semaphore_signal(barrier, inc=1, device_id={"space": lax.rem(space + d, spaces)}, device_id_type=MESH)
        return carry

    lax.fori_loop(1, spaces, greet, 0)
    pl.semaphore_signal(barrier, inc=1, device_id={"sensor": other_core}, device_id_type=MESH)
    for d in range(1, YS):
        pl.semaphore_signal(barrier, inc=1, device_id={"sensor": on_y(d)}, device_id_type=MESH)
    pl.semaphore_wait(barrier, spaces - 1 + 1 + YS - 1)

    for c in range(CHUNKS):

        def start(d, carry, c=c):
            to = on_space(d // XS, lax.rem(d, XS))
            pltpu.make_async_remote_copy(
                src_ref=piece_of(to, c),
                dst_ref=panel.at[c, my_rows, :],
                send_sem=a2a_send.at[c],
                recv_sem=a2a_recv.at[c],
                device_id={"space": to},
                device_id_type=MESH,
            ).start()
            return carry

        lax.fori_loop(1, spaces, start, 0)

    def all_of(c, sem):
        others = panel.at[c, pl.ds(0, params - rows), :]
        pltpu.make_async_copy(others, others, sem).wait()

    tri = blocks * (blocks + 1) // 2
    pack[tri * LANES :, :] = jnp.zeros((pack.shape[0] - tri * LANES, LANES), jnp.float32)
    across = (((1,), (1,)), ((), ()))
    r_copy.wait()
    for c in range(CHUNKS):
        own[c].wait()
        all_of(c, a2a_recv.at[c])
        hi, mid, low = split3(panel[c])
        left = jnp.concatenate([hi, hi, mid, hi, low, mid], axis=1)
        right = jnp.concatenate([hi, mid, hi, low, hi, mid], axis=1)
        at = 0
        for b in range(blocks):
            strip = lax.dot_general(left[b * LANES : (b + 1) * LANES, :], right[b * LANES :, :], across, preferred_element_type=jnp.float32)
            for k in range(blocks - b):
                block = strip[:, k * LANES : (k + 1) * LANES]
                pack[at : at + LANES, :] = block if c == 0 else pack[at : at + LANES, :] + block
                at += LANES
        pieces = depth // LANES
        r_row = jnp.concatenate([r_own[c * pieces + i : c * pieces + i + 1, :] for i in range(pieces)], axis=1)
        rh, rm, rl = split3(jnp.broadcast_to(r_row, (16, depth)))
        r_left = jnp.concatenate([rh, rh, rm, rh, rl, rm], axis=1)
        g = lax.dot_general(r_left, right, across, preferred_element_type=jnp.float32)
        for b in range(blocks):
            pack[at + b : at + b + 1, :] += g[0:1, b * LANES : (b + 1) * LANES]

    half = pack.shape[0] // CORES
    quarter = half // YS
    piece = quarter // ZS

    def remote(src, dst, send, recv, target):
        return pltpu.make_async_remote_copy(src_ref=src, dst_ref=dst, send_sem=send, recv_sem=recv, device_id=target, device_id_type=MESH)

    def run(copies):
        for copy in copies:
            copy.start()
        for copy in copies:
            copy.wait()

    mine = pl.multiple_of(core * half, half)
    theirs = pl.multiple_of((1 - core) * half, half)

    def y_part(yy, base):
        return pl.ds(pl.multiple_of(base + yy * quarter, quarter), quarter)

    def z_part(zz, base=0):
        return pl.ds(pl.multiple_of(base + zz * piece, piece), piece)

    order = (2, 1, 3, 0)
    core_copies = {}
    for d in order:
        yy = lax.rem(y + d, YS)
        core_copies[d] = remote(pack.at[y_part(yy, theirs), :], core_rx.at[d], core_send.at[d], core_recv.at[d], {"sensor": other_core})
        core_copies[d].start()
    y_copies = []
    for d in order:
        part = y_part(lax.rem(y + d, YS), mine)
        core_copies[d].wait_recv()
        if d:
            pack[part, :] += core_rx[d]
            y_copies.append(remote(pack.at[part, :], y_rx.at[d - 1], y_send.at[d - 1], y_recv.at[d - 1], {"sensor": on_y(d)}))
            y_copies[-1].start()
        else:
            y_sum[...] = pack[part, :] + core_rx[d]
    for copy in y_copies:
        copy.wait_recv()
    y_sum[...] += y_rx[0] + y_rx[1] + y_rx[2]

    z_copies = [
        remote(y_sum.at[z_part(lax.rem(z + d, ZS)), :], z_rx.at[d - 1], z_send.at[d - 1], z_recv.at[d - 1], {"space": on_space(d, 0)})
        for d in (4, 3, 5, 2, 6, 1, 7)
    ]
    for copy in z_copies:
        copy.start()
    for copy in z_copies:
        copy.wait_recv()
    total = y_sum[z_part(z), :]
    for d in range(ZS - 1):
        total = total + z_rx[d]
    x_all[x] = total
    x_copies = [
        remote(x_all.at[x], x_all.at[x], x_send.at[d - 1], x_recv.at[d - 1], {"space": on_space(0, d)})
        for d in (2, 1, 3)
    ]
    for copy in x_copies:
        copy.start()
    for copy in x_copies:
        copy.wait_recv()
    total = x_all[0]
    for d in range(1, XS):
        total = total + x_all[d]
    base = mine + y * quarter
    done = out_ref.at[z_part(z, base), :]
    done[...] = total
    zg_copies = [
        remote(done, done, zg_send.at[d - 1], zg_recv.at[d - 1], {"space": on_space(d, 0)})
        for d in (4, 3, 5, 2, 6, 1, 7)
    ]
    for copy in zg_copies:
        copy.start()
    for copy in zg_copies:
        copy.wait_recv()
    mine_done = out_ref.at[y_part(y, mine), :]
    yg_copies = {d: remote(mine_done, mine_done, yg_send.at[d - 1], yg_recv.at[d - 1], {"sensor": on_y(d)}) for d in (2, 1, 3)}
    for copy in yg_copies.values():
        copy.start()
    cg_copies = []
    for d in (0, 1, 3, 2):
        if d:
            yg_copies[d].wait_recv()
        got = out_ref.at[y_part(lax.rem(y - d + YS, YS), mine), :]
        cg_copies.append(remote(got, got, cg_send.at[d], cg_recv.at[d], {"sensor": other_core}))
        cg_copies[-1].start()
    for copy in cg_copies:
        copy.wait_recv()
    for copy in (*core_copies.values(), *y_copies, *z_copies, *x_copies, *zg_copies, *yg_copies.values(), *cg_copies):
        copy.wait_send()
    for c in range(CHUNKS):
        all_of(c, a2a_send.at[c])


def normal_matrix(jacobian, residual):
    rows, local = jacobian.shape
    spaces = ZS * XS
    params, cols = rows * spaces, local // spaces
    blocks = params // LANES
    packed = (blocks * (blocks + 1) // 2 + 1) * LANES
    unit = CORES * YS * ZS * 8
    packed = -(-packed // unit) * unit
    half = packed // CORES
    quarter = half // YS
    piece = quarter // ZS
    f32, dma = jnp.float32, pltpu.SemaphoreType.DMA
    return pl.pallas_call(
        regroup_kernel,
        out_shape=jax.ShapeDtypeStruct((packed, LANES), f32),
        in_specs=[pl.BlockSpec(memory_space=pltpu.HBM), pl.BlockSpec(memory_space=pltpu.HBM)],
        out_specs=pl.BlockSpec(memory_space=pltpu.VMEM),
        scratch_shapes=[
            pltpu.VMEM((CHUNKS, params, cols // CHUNKS), f32),
            pltpu.VMEM((cols // LANES, LANES), f32),
            pltpu.VMEM((packed, LANES), f32),
            pltpu.VMEM((YS, quarter, LANES), f32),
            pltpu.VMEM((YS - 1, quarter, LANES), f32),
            pltpu.VMEM((quarter, LANES), f32),
            pltpu.VMEM((ZS - 1, piece, LANES), f32),
            pltpu.VMEM((XS, piece, LANES), f32),
            dma((CHUNKS,)), dma,
            dma((CHUNKS,)), dma((CHUNKS,)),
            dma((YS,)), dma((YS,)),
            dma((YS - 1,)), dma((YS - 1,)),
            dma((ZS - 1,)), dma((ZS - 1,)),
            dma((XS - 1,)), dma((XS - 1,)),
            dma((ZS - 1,)), dma((ZS - 1,)),
            dma((YS - 1,)), dma((YS - 1,)),
            dma((YS,)), dma((YS,)),
        ],
        compiler_params=pltpu.CompilerParams(collective_id=0, has_side_effects=True, vmem_limit_bytes=58 << 20),
    )(jacobian, residual.reshape(spaces, -1, LANES))


def block_at(b, c, blocks):
    return b * blocks - b * (b - 1) // 2 + (c - b)


def solve_kernel(blocks, packed, damping, x_ref, mat):
    tri = blocks * (blocks + 1) // 2
    wide = blocks + 1
    eye = lax.broadcasted_iota(jnp.int32, (LANES, LANES), 0) == lax.broadcasted_iota(jnp.int32, (LANES, LANES), 1)
    lam = damping[0]
    scale_rows, scale_cols = [], []
    for b in range(blocks):
        at = block_at(b, b, blocks) * LANES
        diag = jnp.where(eye, packed[at : at + LANES, :], 0.0)
        scale_rows.append(lax.rsqrt(jnp.sum(diag, axis=0, keepdims=True)))
        scale_cols.append(lax.rsqrt(jnp.sum(diag, axis=1, keepdims=True)))
    for b in range(blocks):
        for c in range(b, blocks):
            at = block_at(b, c, blocks) * LANES
            v = packed[at : at + LANES, :] * scale_cols[b] * scale_rows[c]
            if b == c:
                v = jnp.where(eye, 1.0 + lam, v)
            mat[b * LANES : (b + 1) * LANES, c * LANES : (c + 1) * LANES] = v
        g_row = packed[tri * LANES + b : tri * LANES + b + 1, :] * scale_rows[b]
        g_col = jnp.sum(jnp.where(eye, g_row, 0.0), axis=1, keepdims=True)
        mat[b * LANES : (b + 1) * LANES, blocks * LANES :] = jnp.broadcast_to(g_col, (LANES, LANES))

    lane = lax.broadcasted_iota(jnp.int32, (8, LANES), 1)
    sub = lax.broadcasted_iota(jnp.int32, (8, LANES), 0)

    def row(v, i):
        return jnp.broadcast_to(v[i : i + 1, :], (8, LANES))

    def invert(t, own):
        wide_by = PANEL // 8
        for h in range(SLAB // PANEL):
            mine = range(h * wide_by, (h + 1) * wide_by)
            first = own + h * PANEL

            def column(v, q):
                return jnp.broadcast_to(v[:, first + q : first + q + 1], (8, LANES))

            cols = [[column(t[i], q) for i in mine] for q in range(PANEL)]
            rows_of = [t[i] for i in mine]
            for p in range(0, PANEL, 2):
                g, k = divmod(p, 8)
                at, bt, ct = row(cols[p][g], k), row(cols[p + 1][g], k), row(cols[p + 1][g], k + 1)
                r = pltpu.reciprocal(at * ct - bt * bt, approx=True)
                if p == 0:
                    tie = r * 0.0
                av, bv, cv = at * r, bt * r, ct * r
                left, right = list(cols[p]), list(cols[p + 1])
                left[g] = left[g] - jnp.where(sub == k, 1.0, 0.0)
                right[g] = right[g] - jnp.where(sub == k + 1, 1.0, 0.0)
                by0 = [x * cv - y * bv for x, y in zip(left, right)]
                by1 = [y * av - x * bv for x, y in zip(left, right)]

                def eliminate(z):
                    z0, z1 = row(z[g], k), row(z[g], k + 1)
                    return [v - (x * z0 + y * z1) for v, x, y in zip(z, by0, by1)]

                for q in range(p + 2, PANEL):
                    cols[q] = eliminate(cols[q])
                rows_of = eliminate(rows_of)
            u_rows = [row(rows_of[q // 8], q % 8) for q in range(PANEL)]
            others = {i: t[i] + tie for i in range(SLAB // 8) if i not in mine}
            parts = {i: [] for i in others}
            for q in range(PANEL):
                for i in others:
                    parts[i].append(column(others[i], q) * u_rows[q])
            new = []
            for i in range(SLAB // 8):
                if i in mine:
                    new.append(rows_of[i - mine[0]])
                    continue
                while len(parts[i]) > 1:
                    parts[i] = [x + y for x, y in zip(parts[i][::2], parts[i][1::2])]
                new.append(t[i] - parts[i][0])
            t = new
        return t

    def slab_step(b, inner):
        top = b * LANES + inner * SLAB
        own = inner * SLAB
        rest = LANES - SLAB - own
        s = mat[top : top + SLAB, b * LANES :]
        t = []
        for i in range(SLAB // 8):
            unit = jnp.where(lane == sub + (rest + 8 * i), 1.0, 0.0)
            t.append(jnp.where((lane >= own) & (lane < own + SLAB), s[8 * i : 8 * i + 8, :LANES], unit))
        inv = jnp.concatenate(invert(t, own), axis=0)
        skip = LANES if inner else 0
        sh, sm, sl = split3(s[:, skip:])
        ih, im, il = split3(inv)
        weights = jnp.concatenate([ih, ih, im, ih, il, im], axis=0)
        stack = jnp.concatenate([sh, sm, sh, sl, sh, sm], axis=0)
        over = (((0,), (0,)), ((), ()))
        u = lax.dot_general(weights, stack, over, preferred_element_type=jnp.float32)[rest : rest + SLAB, :]
        mat[top : top + SLAB, b * LANES + skip :] = u
        count = (blocks - b) * LANES - skip
        if count == 0:
            return

        def later(v):
            v = v[:, :count]
            if inner:
                return v
            edge = jnp.where(lax.broadcasted_iota(jnp.int32, (SLAB, LANES), 1) >= SLAB, v[:, :LANES], jnp.zeros((SLAB, LANES), v.dtype))
            return edge if count == LANES else jnp.concatenate([edge, v[:, LANES:]], axis=1)

        xh, xm, xl = later(sh), later(sm), later(sl)
        uh, um, ul = split3(u)
        left = jnp.concatenate([xh, xh, xm, xh, xl, xm], axis=0)
        right = jnp.concatenate([uh, um, uh, ul, uh, um], axis=0)
        for o in range(0, count, LANES):
            at = b * LANES + skip + o
            prod = lax.dot_general(left[:, o : o + LANES], right[:, o:], over, preferred_element_type=jnp.float32)
            mat[at : at + LANES, at:] -= prod

    for b in range(blocks):
        for inner in range(LANES // SLAB):
            slab_step(b, inner)

    per = LANES // SLAB
    xs = [jnp.zeros((1, LANES), jnp.float32) for _ in range(blocks)]
    for k in reversed(range(blocks * per)):
        b, inner = divmod(k, per)
        u = mat[k * SLAB : (k + 1) * SLAB, :]
        acc = None
        for t in range(b + (inner == per - 1), blocks):
            term = u[:, t * LANES : (t + 1) * LANES] * xs[t]
            acc = term if acc is None else acc + term
        col = u[:, blocks * LANES :]
        if acc is not None:
            col = col - jnp.sum(acc, axis=1, keepdims=True)
        pick = lax.broadcasted_iota(jnp.int32, (SLAB, LANES), 1) == lax.broadcasted_iota(jnp.int32, (SLAB, LANES), 0) + inner * SLAB
        xs[b] = xs[b] + jnp.sum(jnp.where(pick, col, 0.0), axis=0, keepdims=True)
    for b in range(blocks):
        x_ref[b : b + 1, :] = -(xs[b] * scale_rows[b])


def solve(packed, damping, params):
    blocks = params // LANES
    out = pl.pallas_call(
        functools.partial(solve_kernel, blocks),
        out_shape=jax.ShapeDtypeStruct((blocks, LANES), jnp.float32),
        in_specs=[pl.BlockSpec(memory_space=pltpu.VMEM), pl.BlockSpec(memory_space=pltpu.SMEM)],
        out_specs=pl.BlockSpec(memory_space=pltpu.VMEM),
        scratch_shapes=[pltpu.VMEM((params, params + LANES), jnp.float32)],
        compiler_params=pltpu.CompilerParams(vmem_limit_bytes=58 << 20),
    )(packed, damping)
    return out.reshape(params)


def per_device(jacobian, residual, damping):
    params = jacobian.shape[0] * ZS * XS
    return solve(normal_matrix(jacobian, residual), damping, params)


def solution(mesh):
    placed = (P("space", "sensor"), P("sensor"), P())
    return jax.shard_map(per_device, mesh=mesh, in_specs=placed, out_specs=P(), check_vma=False)
```

time: 101 us -> 85.9 us (0.85)
  Pallas kernels: 98.3 us -> 85.1 us
  local copies, waits for them, and re-layouts: 2.06 us -> 0 us
    pallas_call x1, Pallas kernels: 27.1 us -> 18 us  [solve(): pl.pallas_call(functools.partial(solve_kernel, blocks), out_shape=jax.Sha...]
    pallas_call x1, Pallas kernels: 71.2 us -> 67.1 us  [normal_matrix(): pl.pallas_call(regroup_kernel, out_shape=jax.ShapeDtypeStruct((packed, LA...]
    unnamed x4 -> x0, local copies, waits for them, and re-layouts: 2.06 us -> none
where the time goes in v2:
time: 85.9 us; the launch traced here: 85.7 us
  Pallas kernels  85.1 us (99%)
    pallas_call x1, Pallas kernels, normal_matrix(): pl.pallas_call(regroup_kernel, out_shape=jax.ShapeDtypeStruct((packed, LA...  67.1 us
    pallas_call x1, Pallas kernels, solve(): pl.pallas_call(functools.partial(solve_kernel, blocks), out_shape=jax.Sha...  18 us

profile of v2, /device:TPU:1, one launch (start us, length us, event | category | flops | bytes accessed | tf_op | source)
XLA Modules:
  0.0 85.7 jit_solution(9122767879165530326)
XLA Ops:
  0.7 67.1 %shard_map.37.packed = f32[1536,128]{1,0:T(8,128)} custom-call(f32[16,16384]{1,0:T(8,128)} %j_ref.1, f32[32,4,128]{2,1,0:T(4,128)} %bitcast.2), custom_call_target="tpu_custom_call" | custom-call | tf_op jit(solution)/shard_map/pallas_call | solution.py:220
  67.7 18.0 %shard_map.38 = f32[4,128]{1,0:T(4,128)} custom-call(f32[1536,128]{1,0:T(8,128)} %shard_map.37.packed, f32[1]{0:T(128)S(6)} %copy.4.damping), custom_call_target="tpu_custom_call" | custom-call | tf_op jit(solution)/shard_map/pallas_call | solution.py:390

commit v3 on v2

--- a/solution.py
+++ b/solution.py
@@ -22,9 +22,9 @@
     return hi, mid, low
 
 
-def regroup_kernel(j_ref, r_ref, out_ref, panel, r_own, pack, core_rx, y_rx, y_sum, z_rx, x_all, own_sem, r_sem,
-                   a2a_send, a2a_recv, core_send, core_recv, y_send, y_recv, z_send, z_recv, x_send, x_recv,
-                   zg_send, zg_recv, yg_send, yg_recv, cg_send, cg_recv):
+def regroup_kernel(j_ref, r_ref, out_ref, panel, r_own, pack, core_rx, plane_rx, z_all, own_sem, r_sem,
+                   a2a_send, a2a_recv, core_send, core_recv, plane_send, plane_recv, z_send, z_recv,
+                   back_send, back_recv, last_send, last_recv):
     sensor, space = lax.axis_index("sensor"), lax.axis_index("space")
     y, core = sensor // CORES, sensor % CORES
     z, x = space // XS, space % XS
@@ -38,8 +38,8 @@
     def on_space(dz, dx):
         return lax.rem(z + dz + ZS, ZS) * XS + lax.rem(x + dx + XS, XS)
 
-    def on_y(d):
-        return lax.rem(y + d + YS, YS) * CORES + core
+    def in_plane(dy, dx):
+        return {"sensor": lax.rem(y + dy, YS) * CORES + core, "space": on_space(0, dx)}
 
     other_core = y * CORES + (1 - core)
     my_rows = pl.ds(pl.multiple_of(space * rows, rows), rows)
@@ -61,9 +61,10 @@
 
     lax.fori_loop(1, spaces, greet, 0)
     pl.semaphore_signal(barrier, inc=1, device_id={"sensor": other_core}, device_id_type=MESH)
-    for d in range(1, YS):
-        pl.semaphore_signal(barrier, inc=1, device_id={"sensor": on_y(d)}, device_id_type=MESH)
-    pl.semaphore_wait(barrier, spaces - 1 + 1 + YS - 1)
+    for dy in range(1, YS):
+        for dx in range(XS):
+            pl.semaphore_signal(barrier, inc=1, device_id=in_plane(dy, dx), device_id_type=MESH)
+    pl.semaphore_wait(barrier, spaces - 1 + 1 + (YS - 1) * XS)
 
     for c in range(CHUNKS):
 
@@ -111,95 +112,80 @@
             pack[at + b : at + b + 1, :] += g[0:1, b * LANES : (b + 1) * LANES]
 
     half = pack.shape[0] // CORES
-    quarter = half // YS
-    piece = quarter // ZS
+    strip = half // YS
+    piece = strip // XS
 
     def remote(src, dst, send, recv, target):
         return pltpu.make_async_remote_copy(src_ref=src, dst_ref=dst, send_sem=send, recv_sem=recv, device_id=target, device_id_type=MESH)
 
-    def run(copies):
-        for copy in copies:
-            copy.start()
-        for copy in copies:
-            copy.wait()
-
     mine = pl.multiple_of(core * half, half)
     theirs = pl.multiple_of((1 - core) * half, half)
 
-    def y_part(yy, base):
-        return pl.ds(pl.multiple_of(base + yy * quarter, quarter), quarter)
-
-    def z_part(zz, base=0):
-        return pl.ds(pl.multiple_of(base + zz * piece, piece), piece)
-
+    def strip_of(yy, base):
+        return pl.ds(pl.multiple_of(base + yy * strip, strip), strip)
+
+    def piece_at(yy, xx):
+        return pl.ds(pl.multiple_of(mine + yy * strip + xx * piece, piece), piece)
+
+    sent = []
     order = (2, 1, 3, 0)
     core_copies = {}
-    for d in order:
-        yy = lax.rem(y + d, YS)
-        core_copies[d] = remote(pack.at[y_part(yy, theirs), :], core_rx.at[d], core_send.at[d], core_recv.at[d], {"sensor": other_core})
-        core_copies[d].start()
-    y_copies = []
-    for d in order:
-        part = y_part(lax.rem(y + d, YS), mine)
-        core_copies[d].wait_recv()
-        if d:
-            pack[part, :] += core_rx[d]
-            y_copies.append(remote(pack.at[part, :], y_rx.at[d - 1], y_send.at[d - 1], y_recv.at[d - 1], {"sensor": on_y(d)}))
-            y_copies[-1].start()
-        else:
-            y_sum[...] = pack[part, :] + core_rx[d]
-    for copy in y_copies:
+    for dy in order:
+        core_copies[dy] = remote(pack.at[strip_of(lax.rem(y + dy, YS), theirs), :], core_rx.at[dy], core_send.at[dy], core_recv.at[dy], {"sensor": other_core})
+        core_copies[dy].start()
+    sent += core_copies.values()
+    plane = []
+    for dy in order:
+        to_y = lax.rem(y + dy, YS)
+        core_copies[dy].wait_recv()
+        pack[strip_of(to_y, mine), :] += core_rx[dy]
+        for dx in order:
+            if dy or dx:
+                k = dy * XS + dx - 1
+                plane.append(remote(pack.at[piece_at(to_y, lax.rem(x + dx, XS)), :], plane_rx.at[k], plane_send.at[k], plane_recv.at[k], in_plane(dy, dx)))
+                plane[-1].start()
+    sent += plane
+    for copy in plane:
         copy.wait_recv()
-    y_sum[...] += y_rx[0] + y_rx[1] + y_rx[2]
-
+    parts = [pack[piece_at(y, x), :]] + [plane_rx[k] for k in range(YS * XS - 1)]
+
+    def add_up(parts):
+        while len(parts) > 1:
+            parts = [u + v for u, v in zip(parts[::2], parts[1::2])]
+        return parts[0]
+
+    z_all[z] = add_up(parts)
     z_copies = [
-        remote(y_sum.at[z_part(lax.rem(z + d, ZS)), :], z_rx.at[d - 1], z_send.at[d - 1], z_recv.at[d - 1], {"space": on_space(d, 0)})
+        remote(z_all.at[z], z_all.at[z], z_send.at[d - 1], z_recv.at[d - 1], {"space": on_space(d, 0)})
         for d in (4, 3, 5, 2, 6, 1, 7)
     ]
     for copy in z_copies:
         copy.start()
+    sent += z_copies
     for copy in z_copies:
         copy.wait_recv()
-    total = y_sum[z_part(z), :]
-    for d in range(ZS - 1):
-        total = total + z_rx[d]
-    x_all[x] = total
-    x_copies = [
-        remote(x_all.at[x], x_all.at[x], x_send.at[d - 1], x_recv.at[d - 1], {"space": on_space(0, d)})
-        for d in (2, 1, 3)
-    ]
-    for copy in x_copies:
-        copy.start()
-    for copy in x_copies:
+    done = out_ref.at[piece_at(y, x), :]
+    done[...] = add_up([z_all[i] for i in range(ZS)])
+    back = {}
+    for dy in order:
+        for dx in order:
+            if dy or dx:
+                k = dy * XS + dx - 1
+                back[dy, dx] = remote(done, done, back_send.at[k], back_recv.at[k], in_plane(dy, dx))
+                back[dy, dx].start()
+    sent += back.values()
+    last = []
+    for dy in (0, 1, 3, 2):
+        for dx in order:
+            if dy or dx:
+                back[dy, dx].wait_recv()
+        got = out_ref.at[strip_of(lax.rem(y - dy + YS, YS), mine), :]
+        last.append(remote(got, got, last_send.at[dy], last_recv.at[dy], {"sensor": other_core}))
+        last[-1].start()
+    sent += last
+    for copy in last:
         copy.wait_recv()
-    total = x_all[0]
-    for d in range(1, XS):
-        total = total + x_all[d]
-    base = mine + y * quarter
-    done = out_ref.at[z_part(z, base), :]
-    done[...] = total
-    zg_copies = [
-        remote(done, done, zg_send.at[d - 1], zg_recv.at[d - 1], {"space": on_space(d, 0)})
-        for d in (4, 3, 5, 2, 6, 1, 7)
-    ]
-    for copy in zg_copies:
-        copy.start()
-    for copy in zg_copies:
-        copy.wait_recv()
-    mine_done = out_ref.at[y_part(y, mine), :]
-    yg_copies = {d: remote(mine_done, mine_done, yg_send.at[d - 1], yg_recv.at[d - 1], {"sensor": on_y(d)}) for d in (2, 1, 3)}
-    for copy in yg_copies.values():
-        copy.start()
-    cg_copies = []
-    for d in (0, 1, 3, 2):
-        if d:
-            yg_copies[d].wait_recv()
-        got = out_ref.at[y_part(lax.rem(y - d + YS, YS), mine), :]
-        cg_copies.append(remote(got, got, cg_send.at[d], cg_recv.at[d], {"sensor": other_core}))
-        cg_copies[-1].start()
-    for copy in cg_copies:
-        copy.wait_recv()
-    for copy in (*core_copies.values(), *y_copies, *z_copies, *x_copies, *zg_copies, *yg_copies.values(), *cg_copies):
+    for copy in sent:
         copy.wait_send()
     for c in range(CHUNKS):
         all_of(c, a2a_send.at[c])
@@ -211,34 +197,30 @@
     params, cols = rows * spaces, local // spaces
     blocks = params // LANES
     packed = (blocks * (blocks + 1) // 2 + 1) * LANES
-    unit = CORES * YS * ZS * 8
+    unit = CORES * YS * XS * 8
     packed = -(-packed // unit) * unit
     half = packed // CORES
-    quarter = half // YS
-    piece = quarter // ZS
+    strip = half // YS
+    piece = strip // XS
     f32, dma = jnp.float32, pltpu.SemaphoreType.DMA
     return pl.pallas_call(
         regroup_kernel,
         out_shape=jax.ShapeDtypeStruct((packed, LANES), f32),
-        in_specs=[pl.BlockSpec(memory_space=pltpu.HBM), pl.BlockSpec(memory_space=pltpu.HBM)],
+        in_specs=[pl.BlockSpec(memory_space=pl.ANY), pl.BlockSpec(memory_space=pl.ANY)],
         out_specs=pl.BlockSpec(memory_space=pltpu.VMEM),
         scratch_shapes=[
             pltpu.VMEM((CHUNKS, params, cols // CHUNKS), f32),
             pltpu.VMEM((cols // LANES, LANES), f32),
             pltpu.VMEM((packed, LANES), f32),
-            pltpu.VMEM((YS, quarter, LANES), f32),
-            pltpu.VMEM((YS - 1, quarter, LANES), f32),
-            pltpu.VMEM((quarter, LANES), f32),
-            pltpu.VMEM((ZS - 1, piece, LANES), f32),
-            pltpu.VMEM((XS, piece, LANES), f32),
+            pltpu.VMEM((YS, strip, LANES), f32),
+            pltpu.VMEM((YS * XS - 1, piece, LANES), f32),
+            pltpu.VMEM((ZS, piece, LANES), f32),
             dma((CHUNKS,)), dma,
             dma((CHUNKS,)), dma((CHUNKS,)),
             dma((YS,)), dma((YS,)),
-            dma((YS - 1,)), dma((YS - 1,)),
+            dma((YS * XS - 1,)), dma((YS * XS - 1,)),
             dma((ZS - 1,)), dma((ZS - 1,)),
-            dma((XS - 1,)), dma((XS - 1,)),
-            dma((ZS - 1,)), dma((ZS - 1,)),
-            dma((YS - 1,)), dma((YS - 1,)),
+            dma((YS * XS - 1,)), dma((YS * XS - 1,)),
             dma((YS,)), dma((YS,)),
         ],
         compiler_params=pltpu.CompilerParams(collective_id=0, has_side_effects=True, vmem_limit_bytes=58 << 20),

time: 85.9 us -> 82.2 us (0.957)
  Pallas kernels: 85.1 us -> 81.5 us
    pallas_call x1, Pallas kernels: 67.1 us -> 63.5 us  [normal_matrix(): pl.pallas_call(regroup_kernel, out_shape=jax.ShapeDtypeStruct((packed, LA...]
where the time goes in v3:
time: 82.2 us; the launch traced here: 82.1 us
  Pallas kernels  81.5 us (99%)
    pallas_call x1, Pallas kernels, normal_matrix(): pl.pallas_call(regroup_kernel, out_shape=jax.ShapeDtypeStruct((packed, LA...  63.5 us
    pallas_call x1, Pallas kernels, solve(): pl.pallas_call(functools.partial(solve_kernel, blocks), out_shape=jax.Sha...  18 us

profile of v3, /device:TPU:1, one launch (start us, length us, event | category | flops | bytes accessed | tf_op | source)
XLA Modules:
  0.0 82.1 jit_solution(3334793059358815405)
XLA Ops:
  0.7 63.5 %shard_map.37.packed = f32[1536,128]{1,0:T(8,128)} custom-call(f32[16,16384]{1,0:T(8,128)} %j_ref.1, f32[32,4,128]{2,1,0:T(4,128)} %bitcast.2), custom_call_target="tpu_custom_call" | custom-call | tf_op jit(solution)/shard_map/pallas_call | solution.py:206
  64.1 18.0 %shard_map.38 = f32[4,128]{1,0:T(4,128)} custom-call(f32[1536,128]{1,0:T(8,128)} %shard_map.37.packed, f32[1]{0:T(128)S(6)} %copy.4.damping), custom_call_target="tpu_custom_call" | custom-call | tf_op jit(solution)/shard_map/pallas_call | solution.py:372

commit v4 on v3

--- a/solution.py
+++ b/solution.py
@@ -10,6 +10,7 @@
 MESH = pl.DeviceIdType.MESH
 YS, CORES, ZS, XS = 4, 2, 8, 4
 CHUNKS = 4
+WAVES = 2
 SLAB = 64
 PANEL = 16
 
@@ -112,8 +113,10 @@
             pack[at + b : at + b + 1, :] += g[0:1, b * LANES : (b + 1) * LANES]
 
     half = pack.shape[0] // CORES
-    strip = half // YS
+    wave = half // WAVES
+    strip = wave // YS
     piece = strip // XS
+    waves = range(WAVES)
 
     def remote(src, dst, send, recv, target):
         return pltpu.make_async_remote_copy(src_ref=src, dst_ref=dst, send_sem=send, recv_sem=recv, device_id=target, device_id_type=MESH)
@@ -121,67 +124,69 @@
     mine = pl.multiple_of(core * half, half)
     theirs = pl.multiple_of((1 - core) * half, half)
 
-    def strip_of(yy, base):
-        return pl.ds(pl.multiple_of(base + yy * strip, strip), strip)
-
-    def piece_at(yy, xx):
-        return pl.ds(pl.multiple_of(mine + yy * strip + xx * piece, piece), piece)
-
-    sent = []
-    order = (2, 1, 3, 0)
-    core_copies = {}
-    for dy in order:
-        core_copies[dy] = remote(pack.at[strip_of(lax.rem(y + dy, YS), theirs), :], core_rx.at[dy], core_send.at[dy], core_recv.at[dy], {"sensor": other_core})
-        core_copies[dy].start()
-    sent += core_copies.values()
-    plane = []
-    for dy in order:
-        to_y = lax.rem(y + dy, YS)
-        core_copies[dy].wait_recv()
-        pack[strip_of(to_y, mine), :] += core_rx[dy]
-        for dx in order:
-            if dy or dx:
-                k = dy * XS + dx - 1
-                plane.append(remote(pack.at[piece_at(to_y, lax.rem(x + dx, XS)), :], plane_rx.at[k], plane_send.at[k], plane_recv.at[k], in_plane(dy, dx)))
-                plane[-1].start()
-    sent += plane
-    for copy in plane:
-        copy.wait_recv()
-    parts = [pack[piece_at(y, x), :]] + [plane_rx[k] for k in range(YS * XS - 1)]
+    def strip_of(w, yy, base):
+        return pl.ds(pl.multiple_of(base + w * wave + yy * strip, strip), strip)
+
+    def piece_at(w, yy, xx):
+        return pl.ds(pl.multiple_of(mine + w * wave + yy * strip + xx * piece, piece), piece)
 
     def add_up(parts):
         while len(parts) > 1:
             parts = [u + v for u, v in zip(parts[::2], parts[1::2])]
         return parts[0]
 
-    z_all[z] = add_up(parts)
-    z_copies = [
-        remote(z_all.at[z], z_all.at[z], z_send.at[d - 1], z_recv.at[d - 1], {"space": on_space(d, 0)})
-        for d in (4, 3, 5, 2, 6, 1, 7)
-    ]
-    for copy in z_copies:
-        copy.start()
-    sent += z_copies
-    for copy in z_copies:
-        copy.wait_recv()
-    done = out_ref.at[piece_at(y, x), :]
-    done[...] = add_up([z_all[i] for i in range(ZS)])
+    sent = []
+    order = (2, 1, 3, 0)
+    offsets = [(dy, dx) for dy in order for dx in order if dy or dx]
+    core_copies = {}
+    for w in waves:
+        for dy in order:
+            at = strip_of(w, lax.rem(y + dy, YS), theirs)
+            core_copies[w, dy] = remote(pack.at[at, :], core_rx.at[w, dy], core_send.at[w, dy], core_recv.at[w, dy], {"sensor": other_core})
+            core_copies[w, dy].start()
+    sent += core_copies.values()
+    plane = {}
+    for w in waves:
+        for dy in order:
+            to_y = lax.rem(y + dy, YS)
+            core_copies[w, dy].wait_recv()
+            pack[strip_of(w, to_y, mine), :] += core_rx[w, dy]
+            for dx in order:
+                if dy or dx:
+                    k = dy * XS + dx - 1
+                    source = pack.at[piece_at(w, to_y, lax.rem(x + dx, XS)), :]
+                    plane[w, k] = remote(source, plane_rx.at[w, k], plane_send.at[w, k], plane_recv.at[w, k], in_plane(dy, dx))
+                    plane[w, k].start()
+    sent += plane.values()
+    z_copies = {}
+    for w in waves:
+        for k in range(YS * XS - 1):
+            plane[w, k].wait_recv()
+        z_all[w, z] = add_up([pack[piece_at(w, y, x), :]] + [plane_rx[w, k] for k in range(YS * XS - 1)])
+        for d in (4, 3, 5, 2, 6, 1, 7):
+            z_copies[w, d] = remote(z_all.at[w, z], z_all.at[w, z], z_send.at[w, d - 1], z_recv.at[w, d - 1], {"space": on_space(d, 0)})
+            z_copies[w, d].start()
+    sent += z_copies.values()
     back = {}
-    for dy in order:
-        for dx in order:
-            if dy or dx:
-                k = dy * XS + dx - 1
-                back[dy, dx] = remote(done, done, back_send.at[k], back_recv.at[k], in_plane(dy, dx))
-                back[dy, dx].start()
+    for w in waves:
+        for d in range(1, ZS):
+            z_copies[w, d].wait_recv()
+        done = out_ref.at[piece_at(w, y, x), :]
+        done[...] = add_up([z_all[w, i] for i in range(ZS)])
+        for dy, dx in offsets:
+            k = dy * XS + dx - 1
+            back[w, dy, dx] = remote(done, done, back_send.at[w, k], back_recv.at[w, k], in_plane(dy, dx))
+            back[w, dy, dx].start()
     sent += back.values()
     last = []
-    for dy in (0, 1, 3, 2):
-        for dx in order:
-            if dy or dx:
-                back[dy, dx].wait_recv()
-        got = out_ref.at[strip_of(lax.rem(y - dy + YS, YS), mine), :]
-        last.append(remote(got, got, last_send.at[dy], last_recv.at[dy], {"sensor": other_core}))
-        last[-1].start()
+    for w in waves:
+        for dy in (0, 1, 3, 2):
+            for dx in order:
+                if dy or dx:
+                    back[w, dy, dx].wait_recv()
+            got = out_ref.at[strip_of(w, lax.rem(y - dy + YS, YS), mine), :]
+            last.append(remote(got, got, last_send.at[w, dy], last_recv.at[w, dy], {"sensor": other_core}))
+            last[-1].start()
     sent += last
     for copy in last:
         copy.wait_recv()
@@ -197,33 +202,33 @@
     params, cols = rows * spaces, local // spaces
     blocks = params // LANES
     packed = (blocks * (blocks + 1) // 2 + 1) * LANES
-    unit = CORES * YS * XS * 8
+    unit = CORES * WAVES * YS * XS * 8
     packed = -(-packed // unit) * unit
-    half = packed // CORES
-    strip = half // YS
+    strip = packed // (CORES * WAVES * YS)
     piece = strip // XS
+    others = YS * XS - 1
     f32, dma = jnp.float32, pltpu.SemaphoreType.DMA
     return pl.pallas_call(
         regroup_kernel,
-        out_shape=jax.ShapeDtypeStruct((packed, LANES), f32),
+        out_shape=pltpu.VMEM((packed, LANES), f32),
         in_specs=[pl.BlockSpec(memory_space=pl.ANY), pl.BlockSpec(memory_space=pl.ANY)],
         out_specs=pl.BlockSpec(memory_space=pltpu.VMEM),
         scratch_shapes=[
             pltpu.VMEM((CHUNKS, params, cols // CHUNKS), f32),
             pltpu.VMEM((cols // LANES, LANES), f32),
             pltpu.VMEM((packed, LANES), f32),
-            pltpu.VMEM((YS, strip, LANES), f32),
-            pltpu.VMEM((YS * XS - 1, piece, LANES), f32),
-            pltpu.VMEM((ZS, piece, LANES), f32),
+            pltpu.VMEM((WAVES, YS, strip, LANES), f32),
+            pltpu.VMEM((WAVES, others, piece, LANES), f32),
+            pltpu.VMEM((WAVES, ZS, piece, LANES), f32),
             dma((CHUNKS,)), dma,
             dma((CHUNKS,)), dma((CHUNKS,)),
-            dma((YS,)), dma((YS,)),
-            dma((YS * XS - 1,)), dma((YS * XS - 1,)),
-            dma((ZS - 1,)), dma((ZS - 1,)),
-            dma((YS * XS - 1,)), dma((YS * XS - 1,)),
-            dma((YS,)), dma((YS,)),
+            dma((WAVES, YS)), dma((WAVES, YS)),
+            dma((WAVES, others)), dma((WAVES, others)),
+            dma((WAVES, ZS - 1)), dma((WAVES, ZS - 1)),
+            dma((WAVES, others)), dma((WAVES, others)),
+            dma((WAVES, YS)), dma((WAVES, YS)),
         ],
-        compiler_params=pltpu.CompilerParams(collective_id=0, has_side_effects=True, vmem_limit_bytes=58 << 20),
+        compiler_params=pltpu.CompilerParams(collective_id=0, has_side_effects=True, vmem_limit_bytes=56 << 20),
     )(jacobian, residual.reshape(spaces, -1, LANES))
 
 
@@ -375,7 +380,7 @@
         in_specs=[pl.BlockSpec(memory_space=pltpu.VMEM), pl.BlockSpec(memory_space=pltpu.SMEM)],
         out_specs=pl.BlockSpec(memory_space=pltpu.VMEM),
         scratch_shapes=[pltpu.VMEM((params, params + LANES), jnp.float32)],
-        compiler_params=pltpu.CompilerParams(vmem_limit_bytes=58 << 20),
+        compiler_params=pltpu.CompilerParams(vmem_limit_bytes=24 << 20),
     )(packed, damping)
     return out.reshape(params)
 

time: 82.2 us -> 77.9 us (0.948)
  Pallas kernels: 81.5 us -> 77.1 us
    pallas_call x1, Pallas kernels: 63.5 us -> 60.1 us  [normal_matrix(): pl.pallas_call(regroup_kernel, out_shape=pltpu.VMEM((packed, LANES), f32)...]
    pallas_call x1, Pallas kernels: 18 us -> 17.1 us  [solve(): pl.pallas_call(functools.partial(solve_kernel, blocks), out_shape=jax.Sha...]
where the time goes in v4:
time: 77.9 us; the launch traced here: 77.8 us
  Pallas kernels  77.1 us (99%)
    pallas_call x1, Pallas kernels, normal_matrix(): pl.pallas_call(regroup_kernel, out_shape=pltpu.VMEM((packed, LANES), f32)...  60.1 us
    pallas_call x1, Pallas kernels, solve(): pl.pallas_call(functools.partial(solve_kernel, blocks), out_shape=jax.Sha...  17.1 us

profile of v4, /device:TPU:1, one launch (start us, length us, event | category | flops | bytes accessed | tf_op | source)
XLA Modules:
  0.0 77.8 jit_solution(10844152347751919915)
XLA Ops:
  0.7 60.1 %shard_map.37.packed = f32[1536,128]{1,0:T(8,128)S(1)} custom-call(f32[16,16384]{1,0:T(8,128)} %j_ref.1, f32[32,4,128]{2,1,0:T(4,128)} %bitcast.2), custom_call_target="tpu_custom_call" | custom-call | tf_op jit(solution)/shard_map/pallas_call | solution.py:211
  60.8 17.1 %shard_map.38 = f32[4,128]{1,0:T(4,128)} custom-call(f32[1536,128]{1,0:T(8,128)S(1)} %shard_map.37.packed, f32[1]{0:T(128)S(6)} %copy.4.damping), custom_call_target="tpu_custom_call" | custom-call | tf_op jit(solution)/shard_map/pallas_call | solution.py:377

commit v5 on v4

--- a/solution.py
+++ b/solution.py
@@ -10,7 +10,6 @@
 MESH = pl.DeviceIdType.MESH
 YS, CORES, ZS, XS = 4, 2, 8, 4
 CHUNKS = 4
-WAVES = 2
 SLAB = 64
 PANEL = 16
 
@@ -21,6 +20,16 @@
     mid = rest.astype(jnp.bfloat16)
     low = (rest - mid.astype(jnp.float32)).astype(jnp.bfloat16)
     return hi, mid, low
+
+
+def block_at(b, c, blocks):
+    return b * blocks - b * (b - 1) // 2 + (c - b)
+
+
+def wave_pieces(packed):
+    total = packed // (CORES * YS * XS)
+    first = -(-total // 16) * 8
+    return first, total - first
 
 
 def regroup_kernel(j_ref, r_ref, out_ref, panel, r_own, pack, core_rx, plane_rx, z_all, own_sem, r_sem,
@@ -87,8 +96,6 @@
         others = panel.at[c, pl.ds(0, params - rows), :]
         pltpu.make_async_copy(others, others, sem).wait()
 
-    tri = blocks * (blocks + 1) // 2
-    pack[tri * LANES :, :] = jnp.zeros((pack.shape[0] - tri * LANES, LANES), jnp.float32)
     across = (((1,), (1,)), ((), ()))
     r_copy.wait()
     for c in range(CHUNKS):
@@ -109,14 +116,18 @@
         rh, rm, rl = split3(jnp.broadcast_to(r_row, (16, depth)))
         r_left = jnp.concatenate([rh, rh, rm, rh, rl, rm], axis=1)
         g = lax.dot_general(r_left, right, across, preferred_element_type=jnp.float32)
-        for b in range(blocks):
-            pack[at + b : at + b + 1, :] += g[0:1, b * LANES : (b + 1) * LANES]
+        g_row = g[0:1, :] if c == 0 else g_row + g[0:1, :]
+    lane = lax.broadcasted_iota(jnp.int32, (1, LANES), 1)
+    for b in range(blocks):
+        end = (block_at(b, b, blocks) + 1) * LANES
+        part = g_row[:, b * LANES : (b + 1) * LANES]
+        pack[end - 1 : end, :] = jnp.where(lane < LANES - 1, part, pack[end - 1 : end, :])
+        pack[end - 2 : end - 1, :] = jnp.where(lane == 0, part[:, LANES - 1 :], pack[end - 2 : end - 1, :])
 
     half = pack.shape[0] // CORES
-    wave = half // WAVES
-    strip = wave // YS
-    piece = strip // XS
-    waves = range(WAVES)
+    pieces = wave_pieces(pack.shape[0])
+    waves = range(len(pieces))
+    starts = [sum(pieces[:w]) * YS * XS for w in waves]
 
     def remote(src, dst, send, recv, target):
         return pltpu.make_async_remote_copy(src_ref=src, dst_ref=dst, send_sem=send, recv_sem=recv, device_id=target, device_id_type=MESH)
@@ -125,73 +136,63 @@
     theirs = pl.multiple_of((1 - core) * half, half)
 
     def strip_of(w, yy, base):
-        return pl.ds(pl.multiple_of(base + w * wave + yy * strip, strip), strip)
+        strip = pieces[w] * XS
+        return pl.ds(pl.multiple_of(base + starts[w] + yy * strip, 8), strip)
 
     def piece_at(w, yy, xx):
-        return pl.ds(pl.multiple_of(mine + w * wave + yy * strip + xx * piece, piece), piece)
+        return pl.ds(pl.multiple_of(mine + starts[w] + (yy * XS + xx) * pieces[w], 8), pieces[w])
 
     def add_up(parts):
         while len(parts) > 1:
             parts = [u + v for u, v in zip(parts[::2], parts[1::2])]
         return parts[0]
 
-    sent = []
+    def wait_for(region, sem):
+        pltpu.make_async_copy(region, region, sem).wait()
+
     order = (2, 1, 3, 0)
     offsets = [(dy, dx) for dy in order for dx in order if dy or dx]
     core_copies = {}
     for w in waves:
         for dy in order:
             at = strip_of(w, lax.rem(y + dy, YS), theirs)
-            core_copies[w, dy] = remote(pack.at[at, :], core_rx.at[w, dy], core_send.at[w, dy], core_recv.at[w, dy], {"sensor": other_core})
+            core_copies[w, dy] = remote(pack.at[at, :], core_rx.at[w, dy, pl.ds(0, pieces[w] * XS), :], core_send, core_recv.at[w, dy], {"sensor": other_core})
             core_copies[w, dy].start()
-    sent += core_copies.values()
-    plane = {}
     for w in waves:
         for dy in order:
             to_y = lax.rem(y + dy, YS)
             core_copies[w, dy].wait_recv()
-            pack[strip_of(w, to_y, mine), :] += core_rx[w, dy]
+            pack[strip_of(w, to_y, mine), :] += core_rx[w, dy, : pieces[w] * XS, :]
             for dx in order:
                 if dy or dx:
-                    k = dy * XS + dx - 1
                     source = pack.at[piece_at(w, to_y, lax.rem(x + dx, XS)), :]
-                    plane[w, k] = remote(source, plane_rx.at[w, k], plane_send.at[w, k], plane_recv.at[w, k], in_plane(dy, dx))
-                    plane[w, k].start()
-    sent += plane.values()
-    z_copies = {}
-    for w in waves:
-        for k in range(YS * XS - 1):
-            plane[w, k].wait_recv()
-        z_all[w, z] = add_up([pack[piece_at(w, y, x), :]] + [plane_rx[w, k] for k in range(YS * XS - 1)])
+                    landing = plane_rx.at[w, dy * XS + dx - 1, pl.ds(0, pieces[w]), :]
+                    remote(source, landing, plane_send.at[w], plane_recv.at[w], in_plane(dy, dx)).start()
+    for w in waves:
+        wait_for(plane_rx.at[w, :, pl.ds(0, pieces[w]), :], plane_recv.at[w])
+        z_all[w, z, : pieces[w], :] = add_up([pack[piece_at(w, y, x), :]] + [plane_rx[w, k, : pieces[w], :] for k in range(YS * XS - 1)])
         for d in (4, 3, 5, 2, 6, 1, 7):
-            z_copies[w, d] = remote(z_all.at[w, z], z_all.at[w, z], z_send.at[w, d - 1], z_recv.at[w, d - 1], {"space": on_space(d, 0)})
-            z_copies[w, d].start()
-    sent += z_copies.values()
-    back = {}
-    for w in waves:
-        for d in range(1, ZS):
-            z_copies[w, d].wait_recv()
+            own_slot = z_all.at[w, z, pl.ds(0, pieces[w]), :]
+            remote(own_slot, own_slot, z_send.at[w], z_recv.at[w], {"space": on_space(d, 0)}).start()
+    for w in waves:
+        wait_for(z_all.at[w, pl.ds(0, ZS - 1), pl.ds(0, pieces[w]), :], z_recv.at[w])
         done = out_ref.at[piece_at(w, y, x), :]
-        done[...] = add_up([z_all[w, i] for i in range(ZS)])
+        done[...] = add_up([z_all[w, i, : pieces[w], :] for i in range(ZS)])
         for dy, dx in offsets:
-            k = dy * XS + dx - 1
-            back[w, dy, dx] = remote(done, done, back_send.at[w, k], back_recv.at[w, k], in_plane(dy, dx))
-            back[w, dy, dx].start()
-    sent += back.values()
-    last = []
+            remote(done, done, back_send.at[w], back_recv.at[w, dy], in_plane(dy, dx)).start()
     for w in waves:
         for dy in (0, 1, 3, 2):
-            for dx in order:
-                if dy or dx:
-                    back[w, dy, dx].wait_recv()
+            wait_for(plane_rx.at[w, pl.ds(0, XS if dy else XS - 1), pl.ds(0, pieces[w]), :], back_recv.at[w, dy])
             got = out_ref.at[strip_of(w, lax.rem(y - dy + YS, YS), mine), :]
-            last.append(remote(got, got, last_send.at[w, dy], last_recv.at[w, dy], {"sensor": other_core}))
-            last[-1].start()
-    sent += last
-    for copy in last:
-        copy.wait_recv()
-    for copy in sent:
-        copy.wait_send()
+            remote(got, got, last_send, last_recv, {"sensor": other_core}).start()
+    my_half, other_half = out_ref.at[pl.ds(mine, half), :], out_ref.at[pl.ds(theirs, half), :]
+    wait_for(other_half, last_recv)
+    wait_for(my_half, last_send)
+    wait_for(my_half, core_send)
+    for w in waves:
+        wait_for(plane_rx.at[w, :, pl.ds(0, pieces[w]), :], plane_send.at[w])
+        wait_for(z_all.at[w, pl.ds(0, ZS - 1), pl.ds(0, pieces[w]), :], z_send.at[w])
+        wait_for(plane_rx.at[w, :, pl.ds(0, pieces[w]), :], back_send.at[w])
     for c in range(CHUNKS):
         all_of(c, a2a_send.at[c])
 
@@ -201,11 +202,10 @@
     spaces = ZS * XS
     params, cols = rows * spaces, local // spaces
     blocks = params // LANES
-    packed = (blocks * (blocks + 1) // 2 + 1) * LANES
-    unit = CORES * WAVES * YS * XS * 8
-    packed = -(-packed // unit) * unit
-    strip = packed // (CORES * WAVES * YS)
-    piece = strip // XS
+    packed = blocks * (blocks + 1) // 2 * LANES
+    piece = max(wave_pieces(packed))
+    strip = piece * XS
+    waves = len(wave_pieces(packed))
     others = YS * XS - 1
     f32, dma = jnp.float32, pltpu.SemaphoreType.DMA
     return pl.pallas_call(
@@ -217,29 +217,27 @@
             pltpu.VMEM((CHUNKS, params, cols // CHUNKS), f32),
             pltpu.VMEM((cols // LANES, LANES), f32),
             pltpu.VMEM((packed, LANES), f32),
-            pltpu.VMEM((WAVES, YS, strip, LANES), f32),
-            pltpu.VMEM((WAVES, others, piece, LANES), f32),
-            pltpu.VMEM((WAVES, ZS, piece, LANES), f32),
+            pltpu.VMEM((waves, YS, strip, LANES), f32),
+            pltpu.VMEM((waves, others, piece, LANES), f32),
+            pltpu.VMEM((waves, ZS, piece, LANES), f32),
             dma((CHUNKS,)), dma,
             dma((CHUNKS,)), dma((CHUNKS,)),
-            dma((WAVES, YS)), dma((WAVES, YS)),
-            dma((WAVES, others)), dma((WAVES, others)),
-            dma((WAVES, ZS - 1)), dma((WAVES, ZS - 1)),
-            dma((WAVES, others)), dma((WAVES, others)),
-            dma((WAVES, YS)), dma((WAVES, YS)),
+            dma, dma((waves, YS)),
+            dma((waves,)), dma((waves,)),
+            dma((waves,)), dma((waves,)),
+            dma((waves,)), dma((waves, YS)),
+            dma, dma,
         ],
         compiler_params=pltpu.CompilerParams(collective_id=0, has_side_effects=True, vmem_limit_bytes=56 << 20),
     )(jacobian, residual.reshape(spaces, -1, LANES))
 
 
-def block_at(b, c, blocks):
-    return b * blocks - b * (b - 1) // 2 + (c - b)
-
-
 def solve_kernel(blocks, packed, damping, x_ref, mat):
-    tri = blocks * (blocks + 1) // 2
     wide = blocks + 1
-    eye = lax.broadcasted_iota(jnp.int32, (LANES, LANES), 0) == lax.broadcasted_iota(jnp.int32, (LANES, LANES), 1)
+    deep = lax.broadcasted_iota(jnp.int32, (LANES, LANES), 0)
+    across = lax.broadcasted_iota(jnp.int32, (LANES, LANES), 1)
+    wide_lane = lax.broadcasted_iota(jnp.int32, (1, LANES), 1)
+    eye = deep == across
     lam = damping[0]
     scale_rows, scale_cols = [], []
     for b in range(blocks):
@@ -250,12 +248,18 @@
     for b in range(blocks):
         for c in range(b, blocks):
             at = block_at(b, c, blocks) * LANES
-            v = packed[at : at + LANES, :] * scale_cols[b] * scale_rows[c]
+            v = packed[at : at + LANES, :]
+            if b == c:
+                g_row = jnp.where(wide_lane < LANES - 1, v[LANES - 1 :, :], v[LANES - 2 : LANES - 1, 0:1])
+                last = jnp.sum(jnp.where(eye, v[:, LANES - 1 :], 0.0), axis=0, keepdims=True)
+                v = jnp.where(deep == LANES - 1, last, v)
+                v = jnp.where((deep == LANES - 2) & (across == 0), v[0:1, LANES - 2 : LANES - 1], v)
+            v = v * scale_cols[b] * scale_rows[c]
             if b == c:
                 v = jnp.where(eye, 1.0 + lam, v)
             mat[b * LANES : (b + 1) * LANES, c * LANES : (c + 1) * LANES] = v
-        g_row = packed[tri * LANES + b : tri * LANES + b + 1, :] * scale_rows[b]
-        g_col = jnp.sum(jnp.where(eye, g_row, 0.0), axis=1, keepdims=True)
+            if b == c:
+                g_col = jnp.sum(jnp.where(eye, g_row * scale_rows[b], 0.0), axis=1, keepdims=True)
         mat[b * LANES : (b + 1) * LANES, blocks * LANES :] = jnp.broadcast_to(g_col, (LANES, LANES))
 
     lane = lax.broadcasted_iota(jnp.int32, (8, LANES), 1)

time: 77.9 us -> 76 us (0.976)
  Pallas kernels: 77.1 us -> 75.3 us
    pallas_call x1, Pallas kernels: 60.1 us -> 58.1 us  [normal_matrix(): pl.pallas_call(regroup_kernel, out_shape=pltpu.VMEM((packed, LANES), f32)...]
where the time goes in v5:
time: 76 us
  Pallas kernels  75.3 us (99%)
    pallas_call x1, Pallas kernels, normal_matrix(): pl.pallas_call(regroup_kernel, out_shape=pltpu.VMEM((packed, LANES), f32)...  58.1 us
    pallas_call x1, Pallas kernels, solve(): pl.pallas_call(functools.partial(solve_kernel, blocks), out_shape=jax.Sha...  17.2 us

profile of v5, /device:TPU:1, one launch (start us, length us, event | category | flops | bytes accessed | tf_op | source)
XLA Modules:
  0.0 76.0 jit_solution(2248466565678236828)
XLA Ops:
  0.7 58.1 %shard_map.37.packed = f32[1280,128]{1,0:T(8,128)S(1)} custom-call(f32[16,16384]{1,0:T(8,128)} %j_ref.1, f32[32,4,128]{2,1,0:T(4,128)} %bitcast.2), custom_call_target="tpu_custom_call" | custom-call | tf_op jit(solution)/shard_map/pallas_call | solution.py:211
  58.8 17.2 %shard_map.38 = f32[4,128]{1,0:T(4,128)} custom-call(f32[1280,128]{1,0:T(8,128)S(1)} %shard_map.37.packed, f32[1]{0:T(128)S(6)} %copy.4.damping), custom_call_target="tpu_custom_call" | custom-call | tf_op jit(solution)/shard_map/pallas_call | solution.py:381

commit v6 on v5

--- a/solution.py
+++ b/solution.py
@@ -28,7 +28,7 @@
 
 def wave_pieces(packed):
     total = packed // (CORES * YS * XS)
-    first = -(-total // 16) * 8
+    first = total // 16 * 8
     return first, total - first
 
 
@@ -96,7 +96,63 @@
         others = panel.at[c, pl.ds(0, params - rows), :]
         pltpu.make_async_copy(others, others, sem).wait()
 
+    half = pack.shape[0] // CORES
+    pieces = wave_pieces(pack.shape[0])
+    waves = range(len(pieces))
+    starts = [sum(pieces[:w]) * YS * XS for w in waves]
+
+    def remote(src, dst, send, recv, target):
+        return pltpu.make_async_remote_copy(src_ref=src, dst_ref=dst, send_sem=send, recv_sem=recv, device_id=target, device_id_type=MESH)
+
+    mine = pl.multiple_of(core * half, half)
+    theirs = pl.multiple_of((1 - core) * half, half)
+
+    def strip_of(w, yy, base):
+        strip = pieces[w] * XS
+        return pl.ds(pl.multiple_of(base + starts[w] + yy * strip, 8), strip)
+
+    def piece_at(w, yy, xx):
+        return pl.ds(pl.multiple_of(mine + starts[w] + (yy * XS + xx) * pieces[w], 8), pieces[w])
+
+    def add_up(parts):
+        while len(parts) > 1:
+            parts = [u + v for u, v in zip(parts[::2], parts[1::2])]
+        return parts[0]
+
+    order = (2, 1, 3, 0)
+    core_copies = {}
+    for w in waves:
+        for dy in order:
+            at = strip_of(w, lax.rem(y + dy, YS), theirs)
+            core_copies[w, dy] = remote(pack.at[at, :], core_rx.at[w, dy, pl.ds(0, pieces[w] * XS), :], core_send, core_recv.at[w, dy], {"sensor": other_core})
+
     across = (((1,), (1,)), ((), ()))
+    lane = lax.broadcasted_iota(jnp.int32, (1, LANES), 1)
+    every = [(b, k) for b in range(blocks) for k in range(b, blocks)]
+    share = len(every) // CORES
+
+    def gram_part(part, left, right, first, g_row):
+        chosen = every[part * share : (part + 1) * share]
+        for b in range(blocks):
+            ks = [k for i, k in chosen if i == b]
+            if not ks:
+                continue
+            term = lax.dot_general(
+                left[b * LANES : (b + 1) * LANES, :],
+                right[ks[0] * LANES : (ks[-1] + 1) * LANES, :],
+                across,
+                preferred_element_type=jnp.float32,
+            )
+            for i, k in enumerate(ks):
+                at = block_at(b, k, blocks) * LANES
+                block = term[:, i * LANES : (i + 1) * LANES]
+                pack[at : at + LANES, :] = block if first else pack[at : at + LANES, :] + block
+            if g_row is not None and b in ks:
+                end = (block_at(b, b, blocks) + 1) * LANES
+                g = g_row[:, b * LANES : (b + 1) * LANES]
+                pack[end - 1 : end, :] = jnp.where(lane < LANES - 1, g, pack[end - 1 : end, :])
+                pack[end - 2 : end - 1, :] = jnp.where(lane == 0, g[:, LANES - 1 :], pack[end - 2 : end - 1, :])
+
     r_copy.wait()
     for c in range(CHUNKS):
         own[c].wait()
@@ -104,60 +160,29 @@
         hi, mid, low = split3(panel[c])
         left = jnp.concatenate([hi, hi, mid, hi, low, mid], axis=1)
         right = jnp.concatenate([hi, mid, hi, low, hi, mid], axis=1)
-        at = 0
-        for b in range(blocks):
-            strip = lax.dot_general(left[b * LANES : (b + 1) * LANES, :], right[b * LANES :, :], across, preferred_element_type=jnp.float32)
-            for k in range(blocks - b):
-                block = strip[:, k * LANES : (k + 1) * LANES]
-                pack[at : at + LANES, :] = block if c == 0 else pack[at : at + LANES, :] + block
-                at += LANES
-        pieces = depth // LANES
-        r_row = jnp.concatenate([r_own[c * pieces + i : c * pieces + i + 1, :] for i in range(pieces)], axis=1)
+        span = depth // LANES
+        r_row = jnp.concatenate([r_own[c * span + i : c * span + i + 1, :] for i in range(span)], axis=1)
         rh, rm, rl = split3(jnp.broadcast_to(r_row, (16, depth)))
         r_left = jnp.concatenate([rh, rh, rm, rh, rl, rm], axis=1)
         g = lax.dot_general(r_left, right, across, preferred_element_type=jnp.float32)
         g_row = g[0:1, :] if c == 0 else g_row + g[0:1, :]
-    lane = lax.broadcasted_iota(jnp.int32, (1, LANES), 1)
-    for b in range(blocks):
-        end = (block_at(b, b, blocks) + 1) * LANES
-        part = g_row[:, b * LANES : (b + 1) * LANES]
-        pack[end - 1 : end, :] = jnp.where(lane < LANES - 1, part, pack[end - 1 : end, :])
-        pack[end - 2 : end - 1, :] = jnp.where(lane == 0, part[:, LANES - 1 :], pack[end - 2 : end - 1, :])
-
-    half = pack.shape[0] // CORES
-    pieces = wave_pieces(pack.shape[0])
-    waves = range(len(pieces))
-    starts = [sum(pieces[:w]) * YS * XS for w in waves]
-
-    def remote(src, dst, send, recv, target):
-        return pltpu.make_async_remote_copy(src_ref=src, dst_ref=dst, send_sem=send, recv_sem=recv, device_id=target, device_id_type=MESH)
-
-    mine = pl.multiple_of(core * half, half)
-    theirs = pl.multiple_of((1 - core) * half, half)
-
-    def strip_of(w, yy, base):
-        strip = pieces[w] * XS
-        return pl.ds(pl.multiple_of(base + starts[w] + yy * strip, 8), strip)
-
-    def piece_at(w, yy, xx):
-        return pl.ds(pl.multiple_of(mine + starts[w] + (yy * XS + xx) * pieces[w], 8), pieces[w])
-
-    def add_up(parts):
-        while len(parts) > 1:
-            parts = [u + v for u, v in zip(parts[::2], parts[1::2])]
-        return parts[0]
+        if c < CHUNKS - 1:
+            for part in range(CORES):
+                gram_part(part, left, right, c == 0, None)
+            continue
+        for me in range(CORES):
+
+            @pl.when(core == me)
+            def _(me=me):
+                gram_part(1 - me, left, right, CHUNKS == 1, g_row)
+                for copy in core_copies.values():
+                    copy.start()
+                gram_part(me, left, right, CHUNKS == 1, g_row)
 
     def wait_for(region, sem):
         pltpu.make_async_copy(region, region, sem).wait()
 
-    order = (2, 1, 3, 0)
     offsets = [(dy, dx) for dy in order for dx in order if dy or dx]
-    core_copies = {}
-    for w in waves:
-        for dy in order:
-            at = strip_of(w, lax.rem(y + dy, YS), theirs)
-            core_copies[w, dy] = remote(pack.at[at, :], core_rx.at[w, dy, pl.ds(0, pieces[w] * XS), :], core_send, core_recv.at[w, dy], {"sensor": other_core})
-            core_copies[w, dy].start()
     for w in waves:
         for dy in order:
             to_y = lax.rem(y + dy, YS)

time: 76 us -> 75.8 us (level)
  no operation moved by 1% of the time
where the time goes in v6:
time: 75.8 us; the launch traced here: 75.7 us
  Pallas kernels  75.1 us (99%)
    pallas_call x1, Pallas kernels, normal_matrix(): pl.pallas_call(regroup_kernel, out_shape=pltpu.VMEM((packed, LANES), f32)...  57.9 us
    pallas_call x1, Pallas kernels, solve(): pl.pallas_call(functools.partial(solve_kernel, blocks), out_shape=jax.Sha...  17.2 us

profile of v6, /device:TPU:1, one launch (start us, length us, event | category | flops | bytes accessed | tf_op | source)
XLA Modules:
  0.0 75.7 jit_solution(13464472313273322569)
XLA Ops:
  0.7 57.9 %shard_map.37.packed = f32[1280,128]{1,0:T(8,128)S(1)} custom-call(f32[16,16384]{1,0:T(8,128)} %j_ref.1, f32[32,4,128]{2,1,0:T(4,128)} %bitcast.2), custom_call_target="tpu_custom_call" | custom-call | tf_op jit(solution)/shard_map/pallas_call | solution.py:236
  58.6 17.2 %shard_map.38 = f32[4,128]{1,0:T(4,128)} custom-call(f32[1280,128]{1,0:T(8,128)S(1)} %shard_map.37.packed, f32[1]{0:T(128)S(6)} %copy.4.damping), custom_call_target="tpu_custom_call" | custom-call | tf_op jit(solution)/shard_map/pallas_call | solution.py:406

commit v7 on v6

--- a/solution.py
+++ b/solution.py
@@ -79,7 +79,8 @@
     for c in range(CHUNKS):
 
         def start(d, carry, c=c):
-            to = on_space(d // XS, lax.rem(d, XS))
+            e = 1 + lax.rem(d + spaces // 2 - 2, spaces - 1)
+            to = on_space(e // XS, lax.rem(e, XS))
             pltpu.make_async_remote_copy(
                 src_ref=piece_of(to, c),
                 dst_ref=panel.at[c, my_rows, :],

time: 75.8 us -> 75.9 us (level)
  no operation moved by 1% of the time
where the time goes in v7:
time: 75.9 us; the launch traced here: 75.8 us
  Pallas kernels  75.1 us (99%)
    pallas_call x1, Pallas kernels, normal_matrix(): pl.pallas_call(regroup_kernel, out_shape=pltpu.VMEM((packed, LANES), f32)...  58 us
    pallas_call x1, Pallas kernels, solve(): pl.pallas_call(functools.partial(solve_kernel, blocks), out_shape=jax.Sha...  17.2 us

profile of v7, /device:TPU:1, one launch (start us, length us, event | category | flops | bytes accessed | tf_op | source)
XLA Modules:
  0.0 75.8 jit_solution(7859815502405825421)
XLA Ops:
  0.7 58.0 %shard_map.37.packed = f32[1280,128]{1,0:T(8,128)S(1)} custom-call(f32[16,16384]{1,0:T(8,128)} %j_ref.1, f32[32,4,128]{2,1,0:T(4,128)} %bitcast.2), custom_call_target="tpu_custom_call" | custom-call | tf_op jit(solution)/shard_map/pallas_call | solution.py:237
  58.6 17.2 %shard_map.38 = f32[4,128]{1,0:T(4,128)} custom-call(f32[1280,128]{1,0:T(8,128)S(1)} %shard_map.37.packed, f32[1]{0:T(128)S(6)} %copy.4.damping), custom_call_target="tpu_custom_call" | custom-call | tf_op jit(solution)/shard_map/pallas_call | solution.py:407
